TPU v7x, 256 devices: a whole 4x4x8 slice. The times are simulated.
256 devices in a mesh: dp: 16 (over x, y_lo, core), shard: 16 (over z, y_hi).
Axes of the slice: x: 4, y: 4 (y_hi: 2, y_lo: 2; y = y_hi * 2 + y_lo), z: 8, core: 2. Of those that a mesh axis runs over, the one named last changes fastest.
Arguments:
- layer_input: bfloat16 [32768, 8192], P(('dp', 'shard')), may hold values from -6 to 6
- queries: bfloat16 [32768, 4096], P(('dp', 'shard')), may hold values from -200 to 200
- key_rows: bfloat16 [32768, 512], P(('dp', 'shard')), may hold values from -6 to 6
- value_weight: bfloat16 [8192, 512], P('shard'), may hold values from -0.0625 to 0.0625
- segment_ids: int32 [256, 128], P(('dp', 'shard')), may hold values from 0 to 31, never falling along the last dimension, each value on 1 to 64 neighbouring positions
- send_order: int32 [256, 128], P(('dp', 'shard')), may hold values from 0 to 127, each once within a row
- out_grad: bfloat16 [32768, 4096], P(('dp', 'shard')), may hold values from -6 to 6
Outputs:
- attended: bfloat16 [32768, 4096], P(('dp', 'shard'))
- query_grad: bfloat16 [32768, 4096], P(('dp', 'shard'))
- key_grad: bfloat16 [32768, 512], P(('dp', 'shard'))
- input_grad: bfloat16 [32768, 8192], P(('dp', 'shard'))
- weight_grad: float32 [8192, 512], P('shard')
Inputs may be any that keep to these rules, and one draw needn't show every extreme that they name: Each device's row of send_order is a permutation of its 128 local rows. `segment_ids`: ids never fall along a device's row; each document has 1 to 64 rows.
All inputs are finite; a program needn't handle non-finite values.
Results may differ from a plain program's by a relative error of at most 0.034.
Values may be sent and summed in bfloat16 or wider, within the bound.
No kernel may reach another device: no remote copies, remote signals or barrier semaphores. Data moves between devices by JAX's collectives and lax.ppermute only.
A program may use at most 128 MiB of HBM per device.

v0:
```python
import jax
import jax.numpy as jnp
from jax import lax
from jax.sharding import PartitionSpec as P

HEADS = 32
KV_HEADS = 4
HD = 128


def attend(query_rows, key_block, value_block, seg_row, grad_rows):
    count = query_rows.shape[0]
    group_size = HEADS // KV_HEADS
    factor = HD ** (-0.5)
    query_four = query_rows.reshape(count, KV_HEADS, group_size, HD)
    key_three = key_block.reshape(count, KV_HEADS, HD)
    value_three = value_block.reshape(count, KV_HEADS, HD)
    grad_four = grad_rows.reshape(count, KV_HEADS, group_size, HD)
    position = jnp.arange(count, dtype=jnp.int32)
    allowed = (seg_row[:, None] == seg_row[None, :]) & (position[None, :] <= position[:, None])
    scores = (
        jnp.einsum("qgrd,kgd->grqk", query_four, key_three, preferred_element_type=jnp.float32)
        * factor
    )
    scores = jnp.where(allowed, scores, -1e30)
    highest = jnp.max(scores, axis=-1, keepdims=True)
    expon = jnp.exp(scores - highest)
    probs = expon / jnp.sum(expon, axis=-1, keepdims=True)
    probs_b = probs.astype(jnp.bfloat16)
    attended = jnp.einsum(
        "grqk,kgd->qgrd", probs_b, value_three, preferred_element_type=jnp.float32
    ).astype(jnp.bfloat16)
    dprob = jnp.einsum("qgrd,kgd->grqk", grad_four, value_three, preferred_element_type=jnp.float32)
    delta = jnp.sum(grad_four.astype(jnp.float32) * attended.astype(jnp.float32), axis=-1)
    delta = jnp.transpose(delta, (1, 2, 0))[..., None]
    dscore = (probs * (dprob - delta)).astype(jnp.bfloat16)
    query_grad = (
        jnp.einsum("grqk,kgd->qgrd", dscore, key_three, preferred_element_type=jnp.float32) * factor
    ).astype(jnp.bfloat16)
    key_grad = (
        jnp.einsum("grqk,qgrd->kgd", dscore, query_four, preferred_element_type=jnp.float32)
        * factor
    ).astype(jnp.bfloat16)
    value_grad = jnp.einsum(
        "grqk,qgrd->kgd", probs_b, grad_four, preferred_element_type=jnp.float32
    ).astype(jnp.bfloat16)
    return (
        attended.reshape(count, -1),
        query_grad.reshape(count, -1),
        key_grad.reshape(count, -1),
        value_grad.reshape(count, -1),
    )


def project(source, value_weight):
    full_weight = lax.all_gather(value_weight, "shard", axis=0, tiled=True)
    values = jnp.dot(source, full_weight, preferred_element_type=jnp.float32).astype(jnp.bfloat16)
    return (values, full_weight, source)


def per_device(layer_input, queries, key_rows, value_weight, segment_ids, send_order, out_grad):
    order = send_order[0]
    sent_q = jnp.take(queries, order, axis=0)
    sent_k = jnp.take(key_rows, order, axis=0)
    sent_x = jnp.take(layer_input, order, axis=0)
    moved_q, moved_k, moved_x = (
        lax.all_to_all(sent_q, "dp", split_axis=0, concat_axis=0, tiled=True),
        lax.all_to_all(sent_k, "dp", split_axis=0, concat_axis=0, tiled=True),
        lax.all_to_all(sent_x, "dp", split_axis=0, concat_axis=0, tiled=True),
    )
    moved_v, full_weight, columns = project(moved_x, value_weight)
    attended, query_grad, key_grad, grad_moved = attend(
        moved_q, moved_k, moved_v, segment_ids[0], out_grad
    )
    input_grad = lax.dot_general(
        grad_moved, full_weight, (((1,), (1,)), ((), ())), preferred_element_type=jnp.float32
    ).astype(jnp.bfloat16)
    partial_grad = lax.psum_scatter(
        lax.dot_general(
            moved_x, grad_moved, (((0,), (0,)), ((), ())), preferred_element_type=jnp.float32
        ),
        "shard",
        scatter_dimension=0,
        tiled=True,
    )
    weight_grad = lax.psum(partial_grad, "dp")
    return (attended, query_grad, key_grad, input_grad, weight_grad)


def solution(mesh):
    placed = (
        P(("dp", "shard"), None),
        P(("dp", "shard"), None),
        P(("dp", "shard"), None),
        P("shard", None),
        P(("dp", "shard"), None),
        P(("dp", "shard"), None),
        P(("dp", "shard"), None),
    )
    return jax.shard_map(
        per_device,
        mesh=mesh,
        in_specs=placed,
        out_specs=(
            P(("dp", "shard"), None),
            P(("dp", "shard"), None),
            P(("dp", "shard"), None),
            P(("dp", "shard"), None),
            P("shard", None),
        ),
        check_vma=False,
    )
```

profile of v0, /device:TPU:1, one launch (start us, length us, event | category | flops | bytes accessed | tf_op | source)
XLA Modules:
  0.0 580.4 jit_solution(16202340739746860038)
XLA Ops:
  7.2 0.7 all-gather.2.cloned.1.call-update
  8.4 1.3 reduce.3
  10.5 1.8 gather_fusion.1
  12.3 0.7 bitcast_select_fusion.4
  13.1 6.8 %all-to-all-start.1 = ((bf16[16,8,512]{2,1,0:T(8,128)(2,1)}), bf16[16,8,512]{2,1,0:T(8,128)(2,1)S(1)}, u32[]{:S(2)}, u32[]{:S(2)}) async-start(bf16[16,8,512]{2,1,0:T(8,128)(2,1)} %bitcast_select_fusion.4), calls=%async_computation.1 | async-start | bytes 262144 | tf_op jit(solution)/shard_map/all_to_all | solution.py:68
  19.9 2.2 gather_fusion.2
  22.1 2.4 bitcast_select_fusion.3
  24.4 3.2 gather_fusion
  27.6 5.7 all-to-all-start.2
  33.3 3.2 bitcast_select_fusion.1
  36.5 12.5 %all-to-all-done.2 = bf16[16,8,4096]{2,1,0:T(8,128)(2,1)S(1)} async-done(((bf16[16,8,4096]{2,1,0:T(8,128)(2,1)}), bf16[16,8,4096]{2,1,0:T(8,128)(2,1)S(1)}, u32[]{:S(2)}, u32[]{:S(2)}) %all-to-all-start.2) | async-done | bytes 1048608 | tf_op jit(solution)/shard_map/all_to_all | solution.py:67
  49.0 5.1 all-to-all-start
  54.2 2.3 copy.29
  56.7 1.2 copy.60
  57.9 3.6 fusion.34
  61.5 2.0 fusion.10
  63.5 17.7 %all-to-all-done = bf16[16,8,8192]{2,1,0:T(8,128)(2,1)} async-done(((bf16[16,8,8192]{2,1,0:T(8,128)(2,1)}), bf16[16,8,8192]{2,1,0:T(8,128)(2,1)}, u32[]{:S(2)}, u32[]{:S(2)}) %all-to-all-start) | async-done | bytes 2097184 | tf_op jit(solution)/shard_map/all_to_all | solution.py:69
  81.2 9.7 %fusion.3 = f32[8192,512]{1,0:T(8,128)} fusion(bf16[128,512]{0,1:T(8,128)(2,1)S(1)} %bitcast.84, bf16[16,8,8192]{2,1,0:T(8,128)(2,1)} %all-to-all-done), kind=kOutput, calls=%fused_computation.9 | convolution fusion | flops 1073741824 | bytes 19005440 | tf_op jit(solution)/shard_map/dot_general | solution.py:79
  91.2 71.2 %all-gather.2.cloned.1.call-done = bf16[8192,512]{1,0:T(8,128)(2,1)} async-done(((bf16[512,512]{1,0:T(8,128)(2,1)}), bf16[8192,512]{1,0:T(8,128)(2,1)}) %all-gather.2.cloned.1.call-update) | async-done | bytes 8388624 | tf_op jit(solution)/shard_map/all_gather | solution.py:56
  162.4 5.3 fusion.11
  167.7 0.7 reshape.96
  168.4 3.3 multiply_reduce_fusion
  172.2 1.7 copy.48
  173.9 272.9 %reduce-scatter.2.cloned.1.call-done = f32[512,512]{1,0:T(8,128)} async-done(((f32[8192,512]{1,0:T(8,128)}), f32[512,512]{1,0:T(8,128)}) %reduce-scatter.2.cloned.1.call-update) | async-done | bytes 1048592 | tf_op jit(solution)/shard_map/reduce_scatter | solution.py:78
  446.9 2.0 fusion.9
  448.9 2.3 copy.37
  451.2 0.8 copy.39
  451.9 1.4 multiply_convert_fusion
  453.3 2.3 copy.38
  455.6 7.6 %convolution_convert_fusion = bf16[128,8192]{1,0:T(8,128)(2,1)} fusion(bf16[128,512]{0,1:T(8,128)(2,1)S(1)} %bitcast.85, bf16[8192,512]{1,0:T(8,128)(2,1)} %all-gather.2.cloned.1.call-done), kind=kOutput, calls=%fused_computation.4 | convolution fusion | flops 1074790400 | bytes 10616832 | tf_op jit(solution)/shard_map/dot_general | solution.py:75
  463.2 108.4 %all-reduce.2.cloned.1.call-done = f32[512,512]{1,0:T(8,128)} async-done(((f32[512,512]{1,0:T(8,128)}), f32[512,512]{1,0:T(8,128)}) %all-reduce.2.cloned.1.call-update) | async-done | bytes 1048592 | tf_op jit(solution)/shard_map/psum | solution.py:86
  571.6 2.3 copy.78
  (33 shorter events, 2.4 us)
Async XLA Ops:
  7.2 17.3 %copy-start = (bf16[128,8192]{1,0:T(8,128)(2,1)S(1)}, bf16[128,8192]{1,0:T(8,128)(2,1)}, u32[]{:S(2)}) copy-start(bf16[128,8192]{1,0:T(8,128)(2,1)} %param.7) | copy-start | bytes 6291460
  7.2 12.7 %copy-start.1 = (bf16[128,4096]{1,0:T(8,128)(2,1)S(1)}, bf16[128,4096]{1,0:T(8,128)(2,1)}, u32[]{:S(2)}) copy-start(bf16[128,4096]{1,0:T(8,128)(2,1)} %param.8) | copy-start | bytes 3145732
  7.2 155.2 %all-gather.2.cloned.1.call-start = ((), (), s32[]{:S(2)}) async-start(), calls=%async_computation.4 | async-start | bytes 8912896 | tf_op jit(solution)/shard_map/all_gather | solution.py:56
  13.1 14.5 %all-to-all-start.1 = ((bf16[16,8,512]{2,1,0:T(8,128)(2,1)}), bf16[16,8,512]{2,1,0:T(8,128)(2,1)S(1)}, u32[]{:S(2)}, u32[]{:S(2)}) async-start(bf16[16,8,512]{2,1,0:T(8,128)(2,1)} %bitcast_select_fusion.4), calls=%async_computation.1 | async-start | bytes 262144 | tf_op jit(solution)/shard_map/all_to_all | solution.py:68
  27.6 21.4 %all-to-all-start.2 = ((bf16[16,8,4096]{2,1,0:T(8,128)(2,1)}), bf16[16,8,4096]{2,1,0:T(8,128)(2,1)S(1)}, u32[]{:S(2)}, u32[]{:S(2)}) async-start(bf16[16,8,4096]{2,1,0:T(8,128)(2,1)} %bitcast_select_fusion.3), calls=%async_computation.2 | async-start | bytes 2097152 | tf_op jit(solution)/shard_map/all_to_all | solution.py:67
  49.0 32.2 %all-to-all-start = ((bf16[16,8,8192]{2,1,0:T(8,128)(2,1)}), bf16[16,8,8192]{2,1,0:T(8,128)(2,1)}, u32[]{:S(2)}, u32[]{:S(2)}) async-start(bf16[16,8,8192]{2,1,0:T(8,128)(2,1)} %bitcast_select_fusion.1), calls=%async_computation | async-start | bytes 4194304 | tf_op jit(solution)/shard_map/all_to_all | solution.py:69
  54.1 2.3 copy-start.5
  54.1 392.7 %reduce-scatter.2.cloned.1.call-start = ((), (), s32[]{:S(2)}) async-start(), calls=%async_computation.5 | async-start | bytes 17825792 | tf_op jit(solution)/shard_map/reduce_scatter | solution.py:78
  57.9 3.6 copy-start.2
  61.5 2.1 copy-start.7
  91.0 77.4 %copy-start.8 = (f32[4,8,128]{2,1,0:T(8,128)S(1)}, f32[4,8,128]{2,1,0:T(8,128)}, u32[]{:S(2)}) copy-start(f32[4,8,128]{2,1,0:T(8,128)} %copy-done.7) | copy-start | bytes 49156
  91.0 480.6 %all-reduce.2.cloned.1.call-start = ((), (), s32[]{:S(2)}) async-start(), calls=%async_computation.6 | async-start | bytes 2097152 | tf_op jit(solution)/shard_map/psum | solution.py:86
  168.4 3.3 copy-start.3
  168.4 3.3 copy-start.4
  168.4 3.3 copy-start.6
Sparse Core Ops, SparseCore 0:
  10.6 151.7 all-gather.1
  166.5 280.2 reduce-scatter.1
  449.5 122.0 all-reduce.1
where the time goes:
time: 581 us; the launch traced here: 580 us
  waiting for transfers between devices  483 us (83%)
  matrix products  35.4 us (6%)
  local copies, waits for them, and re-layouts  21.3 us (4%)
  starting transfers between devices  17.9 us (3%)
  between operations  13.9 us (2%)
  other arithmetic  8.39 us (1%)
    reduce_scatter x1, waiting for transfers between devices, per_device(): lax.psum_scatter(lax.dot_general(moved_x, grad_moved, (((0,), (0,)), ((),...  273 us
    psum x1, waiting for transfers between devices, per_device(): weight_grad = lax.psum(partial_grad, 'dp')  108 us
    all_gather x1, waiting for transfers between devices, project(): full_weight = lax.all_gather(value_weight, 'shard', axis=0, tiled=True)  71.2 us
    all_to_all x1, waiting for transfers between devices, per_device(): lax.all_to_all(sent_x, 'dp', split_axis=0, concat_axis=0, tiled=True)  17.7 us
    all_to_all x1, waiting for transfers between devices, per_device(): lax.all_to_all(sent_q, 'dp', split_axis=0, concat_axis=0, tiled=True)  12.5 us
  transfers between devices with their start and end apart: 6, of which 5 were waited for; matrix products, arithmetic and copies ran while one was open for 11% of the time, Pallas kernels for 0%

commit v1 on v0

v1 whole, which is shorter than its diff:
```python
import jax
import jax.numpy as jnp
from jax import lax
from jax.experimental import pallas as pl
from jax.experimental.pallas import tpu as pltpu
from jax.sharding import Mesh, PartitionSpec as P

HEADS = 32
KV_HEADS = 4
HD = 128
GROUP = HEADS // KV_HEADS
ROWS = 128
D = 8192
KVW = KV_HEADS * HD
HQW = HEADS * HD
N_DP = 16
N_SHARD = 16
SUB = D // N_DP // N_SHARD
FACTOR = HD ** (-0.5)
VMEM = 60 * 1024 * 1024
LIGHT = pl.CostEstimate(flops=0, bytes_accessed=0, transcendentals=0)

FINE = (("x", 4), ("yl", 2), ("c", 2), ("z", 8), ("yh", 2))
DP = ("x", "yl", "c")
SHARD = ("z", "yh")
ALL = DP + SHARD

NT = (((1,), (1,)), ((), ()))
TN = (((0,), (0,)), ((), ()))


def dot(a, b, dims=(((1,), (0,)), ((), ()))):
    return lax.dot_general(a, b, dims, preferred_element_type=jnp.float32)


def swap(size, offset):
    return [(i, i ^ offset) for i in range(size)]


def sort_matrix(order_row):
    local = lax.broadcasted_iota(jnp.int32, (ROWS, ROWS), 0)
    return (local == jnp.broadcast_to(order_row, (ROWS, ROWS))).astype(jnp.bfloat16)


def sort_qk_kernel(order_ref, q_ref, k_ref, out_ref):
    pick = sort_matrix(order_ref[...])
    out_ref[:, :HQW] = dot(pick, q_ref[...], TN).astype(jnp.bfloat16)
    out_ref[:, HQW:] = dot(pick, k_ref[...], TN).astype(jnp.bfloat16)


def sort_qk(order, queries, key_rows):
    return pl.pallas_call(
        sort_qk_kernel,
        out_shape=jax.ShapeDtypeStruct((ROWS, HQW + KVW), jnp.bfloat16),
        cost_estimate=LIGHT,
        compiler_params=pltpu.CompilerParams(vmem_limit_bytes=VMEM),
        name="sort_qk",
    )(order, queries, key_rows)


PEERS = 8
RING = 8
DEAL = 4 * HD


def deal_columns(place_ref, order_ref, x_ref, deal_ref, rows_ref, put):
    @pl.when(pl.program_id(0) == 0)
    def _():
        a = lax.broadcasted_iota(jnp.int32, (DEAL, 2 * HD), 0)
        b = lax.broadcasted_iota(jnp.int32, (DEAL, 2 * HD), 1)
        deal_ref[...] = (
            ((a >> 7) == ((b >> 5) & 3))
            & (((a >> 5) & 3) == (b >> 7) * 2 + place_ref[2])
            & ((a & 31) == (b & 31))
        ).astype(jnp.bfloat16)

    rows_ref[...] = dot(sort_matrix(order_ref[...]), x_ref[...], TN).astype(jnp.bfloat16)
    for t in range(4):
        lanes = [slice(s * KVW + t * HD, s * KVW + (t + 1) * HD) for s in range(4)]
        part = jnp.concatenate([rows_ref[:, one] for one in lanes], axis=1)
        dealt = dot(part, deal_ref[...]).astype(jnp.bfloat16)
        for u in range(2):
            put(t * 2 + u, dealt[:, u * HD : (u + 1) * HD])


def sort_own_kernel(place_ref, order_ref, x_ref, *refs):
    *out_refs, deal_ref, rows_ref, dealt_ref = refs
    here = place_ref[0] * 2 + place_ref[1]

    def put(n, block):
        dealt_ref[here ^ n] = block

    deal_columns(place_ref, order_ref, x_ref, deal_ref, rows_ref, put)
    for k in range(PEERS):
        out_refs[k][...] = dealt_ref[k]


def sort_other_kernel(place_ref, order_ref, x_ref, out_ref, deal_ref, rows_ref):
    def put(n, block):
        out_ref[n] = block

    deal_columns(place_ref, order_ref, x_ref, deal_ref, rows_ref, put)


def sort_x(place, order, x, own):
    scratch = [pltpu.VMEM((DEAL, 2 * HD), jnp.bfloat16), pltpu.VMEM((ROWS, 4 * KVW), jnp.bfloat16)]
    if own:
        out_specs = [pl.BlockSpec((ROWS, HD), lambda i: (0, i))] * PEERS
        out_shape = [jax.ShapeDtypeStruct((ROWS, KVW), jnp.bfloat16)] * PEERS
        scratch.append(pltpu.VMEM((PEERS, ROWS, HD), jnp.bfloat16))
    else:
        out_specs = pl.BlockSpec((PEERS, ROWS, HD), lambda i: (0, 1, i))
        out_shape = jax.ShapeDtypeStruct((PEERS, 2 * ROWS, KVW), jnp.bfloat16)
    return pl.pallas_call(
        sort_own_kernel if own else sort_other_kernel,
        grid=(4,),
        in_specs=[
            pl.BlockSpec(memory_space=pltpu.SMEM),
            pl.BlockSpec((1, ROWS), lambda i: (0, 0)),
            pl.BlockSpec((ROWS, 4 * KVW), lambda i: (0, i)),
        ],
        out_specs=out_specs,
        out_shape=out_shape,
        scratch_shapes=scratch,
        cost_estimate=LIGHT,
        compiler_params=pltpu.CompilerParams(vmem_limit_bytes=VMEM),
        name="sort_own" if own else "sort_other",
    )(place, order, x)


def probs_kernel(seg_ref, q_ref, k_ref, grad_ref, _, probs_ref, value_grad_ref, payload_ref):
    seg_query = jnp.broadcast_to(seg_ref[...], (ROWS, ROWS))
    seg_key = seg_query.T
    key_at = lax.broadcasted_iota(jnp.int32, (ROWS, ROWS), 0)
    query_at = lax.broadcasted_iota(jnp.int32, (ROWS, ROWS), 1)
    allowed = (seg_key == seg_query) & (key_at <= query_at)
    bias = jnp.where(allowed, 0.0, -1e30).astype(jnp.float32)
    total = jnp.zeros((ROWS, HD), jnp.float32)
    for r in range(GROUP):
        head = slice(r * HD, (r + 1) * HD)
        scores = dot(k_ref[...], q_ref[:, head], NT) * FACTOR
        scores = jnp.where(allowed, scores, bias)
        highest = jnp.max(scores, axis=0, keepdims=True)
        expon = jnp.exp(scores - highest)
        probs = expon / jnp.sum(expon, axis=0, keepdims=True)
        probs_ref[:, head] = probs
        total += dot(probs.astype(jnp.bfloat16), grad_ref[:, head])
    total = total.astype(jnp.bfloat16)
    value_grad_ref[...] = total
    for n in range(PEERS):
        payload_ref[n] = total


def make_probs(seg, moved, out_grad, payload):
    wide = GROUP * HD
    return pl.pallas_call(
        probs_kernel,
        grid=(KV_HEADS,),
        in_specs=[
            pl.BlockSpec((1, ROWS), lambda i: (0, 0)),
            pl.BlockSpec((ROWS, wide), lambda i: (0, i)),
            pl.BlockSpec((ROWS, HD), lambda i: (0, HEADS + i)),
            pl.BlockSpec((ROWS, wide), lambda i: (0, i)),
            pl.BlockSpec(memory_space=pl.ANY),
        ],
        out_specs=[
            pl.BlockSpec((ROWS, wide), lambda i: (0, i)),
            pl.BlockSpec((ROWS, HD), lambda i: (0, i)),
            pl.BlockSpec((PEERS, ROWS, HD), lambda i: (0, 0, i)),
        ],
        out_shape=[
            jax.ShapeDtypeStruct((ROWS, HQW), jnp.float32),
            jax.ShapeDtypeStruct((ROWS, KVW), jnp.bfloat16),
            jax.ShapeDtypeStruct(payload.shape, payload.dtype),
        ],
        input_output_aliases={4: 2},
        cost_estimate=LIGHT,
        compiler_params=pltpu.CompilerParams(vmem_limit_bytes=VMEM),
        name="probs",
    )(seg, moved, moved, out_grad, payload)


def attend_kernel(probs_ref, q_ref, k_ref, v_ref, share_ref, grad_ref, *refs):
    attended_ref, query_grad_ref, key_grad_ref, weight_grad_ref, wide_ref = refs
    weight_grad_ref[...] = share_ref[...].reshape(weight_grad_ref.shape).astype(jnp.float32)

    @pl.when(pl.program_id(0) == 0)
    def _():
        wide_ref[...] = v_ref[...].astype(jnp.float32)

    each = ROWS // N_DP
    own = pl.ds(pl.multiple_of(pl.program_id(0) * each, each), each)
    value = jnp.concatenate([wide_ref[source, own, :] for source in range(N_DP)], axis=0).astype(jnp.bfloat16)
    total = jnp.zeros((ROWS, HD), jnp.float32)
    for r in range(GROUP):
        head = slice(r * HD, (r + 1) * HD)
        probs = probs_ref[:, head]
        probs_b = probs.astype(jnp.bfloat16)
        attended_ref[:, head] = dot(probs_b, value, TN).astype(jnp.bfloat16)
        dprob = dot(value, grad_ref[:, head], NT)
        delta = jnp.sum(probs_b.astype(jnp.float32) * dprob, axis=0, keepdims=True)
        dscore = (probs * (dprob - delta)).astype(jnp.bfloat16)
        query_grad_ref[:, head] = (dot(dscore, k_ref[...], TN) * FACTOR).astype(jnp.bfloat16)
        total += dot(dscore, q_ref[:, head])
    key_grad_ref[...] = (total * FACTOR).astype(jnp.bfloat16)


def attend(probs, moved, got, out_grad):
    wide = GROUP * HD
    block = pl.BlockSpec((ROWS, wide), lambda i: (0, i))
    narrow = pl.BlockSpec((ROWS, HD), lambda i: (0, i))
    return pl.pallas_call(
        attend_kernel,
        grid=(KV_HEADS,),
        in_specs=[
            block,
            block,
            pl.BlockSpec((ROWS, HD), lambda i: (0, HEADS + i)),
            pl.BlockSpec((N_DP, SUB, HD), lambda i: (0, 0, KVW // HD)),
            pl.BlockSpec((N_DP // KV_HEADS, SUB, KVW), lambda i: (i, 0, 0)),
            block,
        ],
        out_specs=[block, block, narrow, pl.BlockSpec((KVW // KV_HEADS, KVW), lambda i: (i, 0))],
        scratch_shapes=[pltpu.VMEM((N_DP, SUB, HD), jnp.float32)],
        out_shape=[
            jax.ShapeDtypeStruct((ROWS, HQW), jnp.bfloat16),
            jax.ShapeDtypeStruct((ROWS, HQW), jnp.bfloat16),
            jax.ShapeDtypeStruct((ROWS, KVW), jnp.bfloat16),
            jax.ShapeDtypeStruct((KVW, KVW), jnp.float32),
        ],
        cost_estimate=LIGHT,
        compiler_params=pltpu.CompilerParams(vmem_limit_bytes=VMEM),
        name="attend",
    )(probs, moved, moved, got, got, out_grad)


def weight_kernel(place_ref, *refs):
    x_refs, both_ref, other_ref, out_ref, wide_ref, total_ref = refs[:PEERS], *refs[PEERS:]
    core = place_ref[2]
    here = place_ref[0] * 2 + place_ref[1]
    for k in range(PEERS):
        wide_ref[(here ^ k) * 2 + core] = x_refs[k][...].astype(jnp.float32)
        wide_ref[k * 2 + 1 - core] = both_ref[k, ROWS:, :].astype(jnp.float32)
    for step in range(PEERS // 2):
        lhs, rhs = [], []
        for at in (step * 2, step * 2 + 1):
            for co in range(2):
                to = at * 2 + (core ^ co)
                rows = pl.ds(pl.multiple_of(to * 8, 8), 8)
                lhs += [wide_ref[source, rows, :] for source in range(N_DP)]
                rhs.append(other_ref[at] if co else both_ref[at, :ROWS, :])
        part = dot(jnp.concatenate(lhs, axis=0).astype(jnp.bfloat16), jnp.concatenate(rhs, axis=0), TN)
        if step == 0:
            total_ref[...] = part
        elif step < PEERS // 2 - 1:
            total_ref[...] += part
        else:
            out_ref[...] = (total_ref[...] + part).astype(jnp.bfloat16).reshape(out_ref.shape)


def weight_part(place, rows_x, both, other):
    vmem = pl.BlockSpec(memory_space=pltpu.VMEM)
    return pl.pallas_call(
        weight_kernel,
        in_specs=[pl.BlockSpec(memory_space=pltpu.SMEM)] + [vmem] * (PEERS + 2),
        out_specs=vmem,
        out_shape=jax.ShapeDtypeStruct((N_SHARD, SUB, KVW), jnp.bfloat16),
        scratch_shapes=[
            pltpu.VMEM((N_DP, ROWS, KVW), jnp.float32),
            pltpu.VMEM((KVW, KVW), jnp.float32),
        ],
        cost_estimate=LIGHT,
        compiler_params=pltpu.CompilerParams(vmem_limit_bytes=VMEM),
        name="weight_part",
    )(place, *rows_x, both, other)


def column_blocks(place_ref):
    deep = D // RING // 2
    for k in range(RING):
        z = (place_ref[4] + k) & (RING - 1)
        for n in range(2):
            yield k, pl.ds(n * deep, deep), pl.ds(pl.multiple_of((z * 2 + (place_ref[3] ^ n)) * deep, deep), deep)


def values_kernel(place_ref, order_ref, x_ref, *refs):
    own_refs, other_refs, out_ref = refs[:RING], refs[RING : 2 * RING], refs[2 * RING]
    mine = jnp.zeros((ROWS, KVW // 2), jnp.float32)
    theirs = jnp.zeros((ROWS, KVW // 2), jnp.float32)
    for k, rows, at in column_blocks(place_ref):
        x = x_ref[:, at]
        mine += dot(x, own_refs[k][rows, :])
        theirs += dot(x, other_refs[k][rows, :])
    first = place_ref[2] == 0
    values = jnp.concatenate([jnp.where(first, mine, theirs), jnp.where(first, theirs, mine)], axis=1)
    values = values.astype(jnp.bfloat16)
    order = jnp.broadcast_to(order_ref[...], (ROWS, ROWS)).T
    pick = (order == lax.broadcasted_iota(jnp.int32, (ROWS, ROWS), 1)).astype(jnp.float32)
    each = ROWS // N_DP
    spread = jnp.concatenate(
        [pick[g * each : (g + 1) * each] for g in range(N_DP) for _ in range(KV_HEADS)], axis=0
    )
    head_of = (lax.broadcasted_iota(jnp.int32, spread.shape, 0) >> 3) & 3
    total = jnp.zeros((N_DP * KV_HEADS * each, HD), jnp.float32)
    for i in range(KV_HEADS):
        one = jnp.where(head_of == i, spread, 0.0).astype(jnp.bfloat16)
        total += dot(one, values[:, i * HD : (i + 1) * HD])
    out_ref[...] = total.astype(jnp.bfloat16).reshape(out_ref.shape)


def input_grad_kernel(place_ref, grad_ref, *refs):
    own_refs, other_refs, out_ref = refs[:RING], refs[RING : 2 * RING], refs[2 * RING]
    half = KVW // 2
    core = place_ref[2]
    grads = [grad_ref[:, pl.ds(pl.multiple_of(at * half, half), half)] for at in (core, 1 - core)]
    for k, rows, at in column_blocks(place_ref):
        part = dot(grads[0], own_refs[k][rows, :], NT) + dot(grads[1], other_refs[k][rows, :], NT)
        out_ref[:, at] = part.astype(jnp.bfloat16)


def with_weight(kernel, name, out_shape, place, *operands):
    vmem = pl.BlockSpec(memory_space=pltpu.VMEM)
    return pl.pallas_call(
        kernel,
        in_specs=[pl.BlockSpec(memory_space=pltpu.SMEM)] + [vmem] * len(operands),
        out_specs=vmem,
        out_shape=jax.ShapeDtypeStruct(out_shape, jnp.bfloat16),
        cost_estimate=LIGHT,
        compiler_params=pltpu.CompilerParams(vmem_limit_bytes=VMEM),
        name=name,
    )(place, *operands)


def share_kernel(shares_ref, v_ref, out_ref):
    total = shares_ref[0].astype(jnp.float32)
    for s in range(1, N_SHARD):
        total += shares_ref[s].astype(jnp.float32)
    total = total.astype(jnp.bfloat16)
    for g in range(N_DP):
        out_ref[g, :, :KVW] = total
    out_ref[:, :, KVW:] = v_ref[...]


def make_share(shares, sent_v):
    return pl.pallas_call(
        share_kernel,
        out_shape=jax.ShapeDtypeStruct((N_DP, SUB, KVW + HD), jnp.bfloat16),
        cost_estimate=LIGHT,
        compiler_params=pltpu.CompilerParams(vmem_limit_bytes=VMEM),
        name="share",
    )(shares, sent_v)


def per_device(layer_input, queries, key_rows, value_weight, segment_ids, send_order, out_grad):
    core = lax.axis_index("c")
    place = jnp.stack([lax.axis_index(name) for name in ("x", "yl", "c", "yh", "z")]).astype(jnp.int32)
    peers = ("x", "yl")
    right = [(i, (i + 1) % RING) for i in range(RING)]
    left = [(i, (i - 1) % RING) for i in range(RING)]
    half = lax.dynamic_slice(value_weight, (0, core * (KVW // 2)), (value_weight.shape[0], KVW // 2))
    other = lax.ppermute(half, "yh", swap(2, 1))
    other_x = lax.ppermute(layer_input, "c", swap(2, 1))
    other_order = lax.ppermute(send_order, "c", swap(2, 1))
    sent = sort_qk(send_order, queries, key_rows)
    rows_x = list(sort_x(place, send_order, layer_input, True))
    other, other_order, sent, rows_x = lax.optimization_barrier((other, other_order, sent, rows_x))
    moved = lax.all_to_all(
        sent.reshape(N_DP, ROWS // N_DP, HQW + KVW), DP, split_axis=0, concat_axis=0, tiled=True
    ).reshape(ROWS, HQW + KVW)
    weight = jnp.concatenate([half, other], axis=0)
    up, down = [weight], [weight]
    payload = sort_x(place, other_order, other_x, False)
    payload, rows_x[5:] = lax.optimization_barrier((payload, rows_x[5:]))
    rows_x = rows_x[:1] + [lax.ppermute(rows_x[k], peers, swap(PEERS, k)) for k in range(1, PEERS)]
    up.append(lax.ppermute(up[0], "z", right))
    down.append(lax.ppermute(down[0], "z", left))

    early = 3
    moved, rows_x[:early], up[1], down[1] = lax.optimization_barrier((moved, rows_x[:early], up[1], down[1]))
    probs, value_grad, payload = make_probs(segment_ids, moved, out_grad, payload)

    up.append(lax.ppermute(up[1], "z", right))
    down.append(lax.ppermute(down[1], "z", left))
    payload, rows_x = lax.optimization_barrier((payload, rows_x))
    both = lax.all_to_all(payload, peers, split_axis=0, concat_axis=0, tiled=True)
    up.append(lax.ppermute(up[2], "z", right))
    down.append(lax.ppermute(down[2], "z", left))
    both, up[3], down[3] = lax.optimization_barrier((both, up[3], down[3]))
    other_grads = lax.ppermute(both[:, :ROWS], "c", swap(2, 1))
    partial = weight_part(place, rows_x, both, other_grads)
    partial, up[3] = lax.optimization_barrier((partial, up[3]))
    shares = lax.all_to_all(partial, SHARD, split_axis=0, concat_axis=0, tiled=True)

    up.append(lax.ppermute(up[3], "z", right))
    own = down[:4] + up[4:0:-1]
    other = [lax.ppermute(one, "c", swap(2, 1)) for one in own]
    sent_v = with_weight(
        values_kernel, "values", (N_DP, SUB, HD), place, send_order, layer_input, *own, *other
    )
    input_grad = with_weight(
        input_grad_kernel, "input_grad", (ROWS, D), place, value_grad, *own, *other
    )

    got = lax.all_to_all(make_share(shares, sent_v), DP, split_axis=0, concat_axis=0, tiled=True)
    got, input_grad = lax.optimization_barrier((got, input_grad))
    attended, query_grad, key_grad, weight_grad = attend(probs, moved, got, out_grad)
    return attended, query_grad, key_grad, input_grad, weight_grad


def solution(mesh):
    fine = Mesh(mesh.devices.reshape([n for _, n in FINE]), [name for name, _ in FINE])
    rows, shard = P(ALL, None), P(SHARD, None)
    return jax.shard_map(
        per_device,
        mesh=fine,
        in_specs=(rows, rows, rows, shard, rows, rows, rows),
        out_specs=(rows, rows, rows, rows, shard),
        check_vma=False,
    )
```

time: 581 us -> 157 us (0.27)
  waiting for transfers between devices: 483 us -> 45.9 us
  Pallas kernels: 0 us -> 47.6 us
  starting transfers between devices: 17.9 us -> 57.9 us
  matrix products: 35.4 us -> 0 us
  local copies, waits for them, and re-layouts: 21.3 us -> 4.11 us
  between operations: 13.9 us -> 1.01 us
  other arithmetic: 8.39 us -> 0.03 us
    reduce_scatter x1 -> x0, waiting for transfers between devices: 273 us -> none  [per_device(): lax.psum_scatter(lax.dot_general(moved_x, grad_moved, (((0,), (0,)), ((),...]
    psum x1 -> x0, waiting for transfers between devices: 108 us -> none  [per_device(): weight_grad = lax.psum(partial_grad, 'dp')]
    all_gather x1 -> x0, waiting for transfers between devices: 71.2 us -> none  [project(): full_weight = lax.all_gather(value_weight, 'shard', axis=0, tiled=True)]
    pallas_call x0 -> x9, Pallas kernels: none -> 47.6 us  [the longest x2 13.8 us: with_weight(): pl.pallas_call(kernel, in_specs=[pl.BlockSpec(memory_space=pltpu.SMEM)] +...]
    ppermute x0 -> x26, waiting for transfers between devices: none -> 41.5 us  [the longest x1 11.7 us: per_device(): up.append(lax.ppermute(up[1], 'z', right))]
    ppermute x0 -> x26, starting transfers between devices: none -> 34.6 us  [the longest x7 8.34 us: per_device(): lax.ppermute(rows_x[k], peers, swap(PEERS, k))]
    dot_general x8 -> x0, matrix products: 31.8 us -> none  [the longest x1 9.7 us: per_device(): lax.dot_general(moved_x, grad_moved, (((0,), (0,)), ((), ())), preferred_...]
    all_to_all x3 -> x4, waiting for transfers between devices: 30.2 us -> 4.43 us  [the longest x1 3.37 us: per_device(): lax.all_to_all(make_share(shares, sent_v), DP, split_axis=0, concat_axis=...]
  transfers between devices with their start and end apart: 6 -> 30, of which waited for: 5 -> 10; matrix products, arithmetic and copies ran while one was open for 11% -> 0% of each run, Pallas kernels for 0% -> 23%
where the time goes in v1:
time: 157 us
  starting transfers between devices  57.9 us (37%)
  Pallas kernels  47.6 us (30%)
  waiting for transfers between devices  45.9 us (29%)
  local copies, waits for them, and re-layouts  4.11 us (3%)
    pallas_call x2, Pallas kernels, with_weight(): pl.pallas_call(kernel, in_specs=[pl.BlockSpec(memory_space=pltpu.SMEM)] +...  13.8 us
    ppermute x1, waiting for transfers between devices, per_device(): up.append(lax.ppermute(up[1], 'z', right))  11.7 us
    ppermute x1, waiting for transfers between devices, per_device(): up.append(lax.ppermute(up[2], 'z', right))  10.8 us
    pallas_call x2, Pallas kernels, sort_x(): pl.pallas_call(sort_own_kernel if own else sort_other_kernel, grid=(4,),...  9.79 us
    ppermute x7, waiting for transfers between devices, per_device(): lax.ppermute(rows_x[k], peers, swap(PEERS, k))  9.74 us
    pallas_call x1, Pallas kernels, attend(): pl.pallas_call(attend_kernel, grid=(KV_HEADS,), in_specs=[block, block, p...  9.43 us
    all_to_all x1, starting transfers between devices, per_device(): lax.all_to_all(partial, SHARD, split_axis=0, concat_axis=0, tiled=True)  8.67 us
    ppermute x7, starting transfers between devices, per_device(): lax.ppermute(rows_x[k], peers, swap(PEERS, k))  8.34 us
  transfers between devices with their start and end apart: 30, of which 10 were waited for; matrix products, arithmetic and copies ran while one was open for 0% of the time, Pallas kernels for 23%

profile of v1, /device:TPU:1, one launch (start us, length us, event | category | flops | bytes accessed | tf_op | source)
XLA Modules:
  0.0 156.5 jit_solution(5524558932220955162)
XLA Ops:
  0.6 3.3 %collective-permute-start.6 = (bf16[128,8192]{1,0:T(8,128)(2,1)}, bf16[128,8192]{1,0:T(8,128)(2,1)}, u32[]{:S(2)}, u32[]{:S(2)}) collective-permute-start(bf16[128,8192]{1,0:T(8,128)(2,1)} %x_ref.3), channel_id=1, source_target_pairs={{0,16},{16,0},{1,17},{17,1},{2,18},{18,2},{3,19},{19,3},{4,20},{20... | collective-permute-start | bytes 6291464 | tf_op jit(solution)/shard_map/ppermute | solution.py:362
  4.0 1.5 collective-permute-start
  7.1 4.9 %sort_own.1 = (bf16[128,512]{1,0:T(8,128)(2,1)}, bf16[128,512]{1,0:T(8,128)(2,1)}, bf16[128,512]{1,0:T(8,128)(2,1)}, bf16[128,512]{1,0:T(8,128)(2,1)}, bf16[128,...) custom-call(s32[5]{0:T(128)} %stack.23.place_ref, ...), custom_call_target="tpu_custom_call" | custom-call | tf_op jit(solution)/shard_map/sort_own/pallas_call | solution.py:114
  12.0 2.8 %sort_qk.1 = bf16[128,4608]{1,0:T(8,128)(2,1)} custom-call(s32[1,128]{1,0:T(1,128)} %order_ref.5, bf16[128,4096]{1,0:T(8,128)(2,1)} %q_ref.1, bf16[128,512]{1,0:T(8,128)(2,1)} %k_ref.1), custom_call_target="tpu_custom_call" | custom-call | tf_op jit(solution)/shard_map/sort_qk/pallas_call | solution.py:52
  14.8 4.6 %all-to-all-start = ((bf16[16,8,4608]{2,1,0:T(8,128)(2,1)}), bf16[16,8,4608]{2,1,0:T(8,128)(2,1)S(1)}, u32[]{:S(2)}, u32[]{:S(2)}) async-start(bf16[16,8,4608]{2,1,0:T(8,128)(2,1)} %bitcast.11), calls=%async_computation | async-start | bytes 2359296 | tf_op jit(solution)/shard_map/all_to_all | solution.py:367
  19.4 1.7 %collective-permute-start.4 = (bf16[1024,256]{1,0:T(8,128)(2,1)S(1)}, bf16[1024,256]{1,0:T(8,128)(2,1)}, u32[]{:S(2)}, u32[]{:S(2)}) collective-permute-start(bf16[1024,256]{1,0:T(8,128)(2,1)S(1)} %pad_maximum_fusion.refs_0_), channel_id=1, source_target_pairs={{0,2},{2,4},{4,6},{6,8},{8,10},{10,12},{12,14},{14,0},{1,3},{3,5},... | collective-permute-start | bytes 1572872 | tf_op jit(solution)/shard_map/ppermute | solution.py:375
  21.1 4.0 %collective-permute-start.5 = (bf16[1024,256]{1,0:T(8,128)(2,1)S(1)}, bf16[1024,256]{1,0:T(8,128)(2,1)}, u32[]{:S(2)}, u32[]{:S(2)}) collective-permute-start(bf16[1024,256]{1,0:T(8,128)(2,1)S(1)} %pad_maximum_fusion.refs_0_), channel_id=1, source_target_pairs={{0,14},{2,0},{4,2},{6,4},{8,6},{10,8},{12,10},{14,12},{1,15},{3,1}... | collective-permute-start | bytes 1572872 | tf_op jit(solution)/shard_map/ppermute | solution.py:376
  27.8 4.9 %sort_other.1._ = bf16[8,256,512]{2,1,0:T(8,128)(2,1)} custom-call(s32[5]{0:T(128)} %stack.23.place_ref, s32[1,128]{1,0:T(1,128)} %copy-done.20, bf16[128,8192]{1,0:T(8,128)(2,1)} %collective-permute-done.6.x_ref), custom_call_target="tpu_custom_call" | custom-call | tf_op jit(solution)/shard_map/sort_other/pallas_call | solution.py:114
  32.7 5.1 %collective-permute-done.2.refs_1_ = bf16[128,512]{1,0:T(8,128)(2,1)S(1)} collective-permute-done((bf16[128,512]{1,0:T(8,128)(2,1)}, bf16[128,512]{1,0:T(8,128)(2,1)S(1)}, u32[]{:S(2)}, u32[]{:S(2)}) %collective-permute-start.2) | collective-permute-done | bytes 131104 | tf_op jit(solution)/shard_map/ppermute | solution.py:374
  37.8 2.2 %collective-permute-start.8 = (bf16[128,512]{1,0:T(8,128)(2,1)}, bf16[128,512]{1,0:T(8,128)(2,1)S(1)}, u32[]{:S(2)}, u32[]{:S(2)}) collective-permute-start(bf16[128,512]{1,0:T(8,128)(2,1)} %get-tuple-element.82), channel_id=1, source_target_pairs={{0,128},{32,160},{64,192},{96,224},{128,0},{160,32},{192,64},{224,... | collective-permute-start | bytes 393224 | tf_op jit(solution)/shard_map/ppermute | solution.py:374
  40.8 2.4 %collective-permute-start.11 = (bf16[128,512]{1,0:T(8,128)(2,1)S(1)}, bf16[128,512]{1,0:T(8,128)(2,1)S(1)}, u32[]{:S(2)}, u32[]{:S(2)}) collective-permute-start(bf16[128,512]{1,0:T(8,128)(2,1)S(1)} %copy-done.22), channel_id=1, source_target_pairs={{0,224},{32,192},{64,160},{96,128},{128,96},{160,64},{192,32},{224... | collective-permute-start | bytes 393224 | tf_op jit(solution)/shard_map/ppermute | solution.py:374
  44.5 5.2 %probs.1 = (f32[128,4096]{1,0:T(8,128)}, bf16[128,512]{1,0:T(8,128)(2,1)}, bf16[8,256,512]{2,1,0:T(8,128)(2,1)}) custom-call(s32[1,128]{1,0:T(1,128)} %seg_ref.1, bf16[128,4608]{1,0:T(8,128)(2,1)} %bitcast.7, bf16[128,4608]{1,0:T(8,128)(2,1)} %bitcast.8, bf16[128,4096]{1,0:T(8,128)(2,1)} %grad_ref.3, ...), custom_call_target="tpu_custom_call", output_to_operand_aliasing={{2}: (4, {})} | custom-call | tf_op jit(solution)/shard_map/probs/pallas_call | solution.py:156
  49.8 4.6 %collective-permute-done.11.refs_7_ = bf16[128,512]{1,0:T(8,128)(2,1)S(1)} collective-permute-done((bf16[128,512]{1,0:T(8,128)(2,1)S(1)}, bf16[128,512]{1,0:T(8,128)(2,1)S(1)}, u32[]{:S(2)}, u32[]{:S(2)}) %collective-permute-start.11) | collective-permute-done | bytes 131104 | tf_op jit(solution)/shard_map/ppermute | solution.py:374
  55.1 3.6 %all-to-all-start.1 = ((bf16[8,256,512]{2,1,0:T(8,128)(2,1)}), bf16[8,256,512]{2,1,0:T(8,128)(2,1)S(1)}, u32[]{:S(2)}, u32[]{:S(2)}) async-start(bf16[8,256,512]{2,1,0:T(8,128)(2,1)} %get-tuple-element.94), calls=%async_computation.1 | async-start | bytes 4194304 | tf_op jit(solution)/shard_map/all_to_all | solution.py:385
  58.7 1.4 collective-permute-start.12
  60.1 4.0 %collective-permute-start.14 = (bf16[1024,256]{1,0:T(8,128)(2,1)}, bf16[1024,256]{1,0:T(8,128)(2,1)S(1)}, u32[]{:S(2)}, u32[]{:S(2)}) collective-permute-start(bf16[1024,256]{1,0:T(8,128)(2,1)} %collective-permute-done.5.refs_1_), channel_id=1, source_target_pairs={{0,14},{2,0},{4,2},{6,4},{8,6},{10,8},{12,10},{14,12},{1,15},{3,1}... | collective-permute-start | bytes 1572872 | tf_op jit(solution)/shard_map/ppermute | solution.py:383
  64.1 11.7 %collective-permute-done.12.refs_6_ = bf16[1024,256]{1,0:T(8,128)(2,1)S(1)} collective-permute-done((bf16[1024,256]{1,0:T(8,128)(2,1)}, bf16[1024,256]{1,0:T(8,128)(2,1)S(1)}, u32[]{:S(2)}, u32[]{:S(2)}) %collective-permute-start.12) | collective-permute-done | bytes 524320 | tf_op jit(solution)/shard_map/ppermute | solution.py:382
  75.9 2.7 %collective-permute-start.15 = (bf16[1024,256]{1,0:T(8,128)(2,1)S(1)}, bf16[1024,256]{1,0:T(8,128)(2,1)}, u32[]{:S(2)}, u32[]{:S(2)}) collective-permute-start(bf16[1024,256]{1,0:T(8,128)(2,1)S(1)} %collective-permute-done.14.refs_2_), channel_id=1, source_target_pairs={{0,14},{2,0},{4,2},{6,4},{8,6},{10,8},{12,10},{14,12},{1,15},{3,1}... | collective-permute-start | bytes 1572872 | tf_op jit(solution)/shard_map/ppermute | solution.py:387
  78.5 10.8 %collective-permute-done.13.refs_5_ = bf16[1024,256]{1,0:T(8,128)(2,1)} collective-permute-done((bf16[1024,256]{1,0:T(8,128)(2,1)S(1)}, bf16[1024,256]{1,0:T(8,128)(2,1)}, u32[]{:S(2)}, u32[]{:S(2)}) %collective-permute-start.13) | collective-permute-done | bytes 524320 | tf_op jit(solution)/shard_map/ppermute | solution.py:386
  89.7 2.0 %collective-permute-start.16 = (bf16[8,128,512]{2,1,0:T(8,128)(2,1)S(1)}, bf16[8,128,512]{2,1,0:T(8,128)(2,1)}, u32[]{:S(2)}, u32[]{:S(2)}) collective-permute-start(bf16[8,128,512]{2,1,0:T(8,128)(2,1)S(1)} %slice.3), channel_id=1, source_target_pairs={{0,16},{16,0},{1,17},{17,1},{2,18},{18,2},{3,19},{19,3},{4,20},{20... | collective-permute-start | bytes 3145736 | tf_op jit(solution)/shard_map/ppermute | solution.py:389
  92.3 1.8 %collective-permute-done.16.refs_9_ = bf16[8,128,512]{2,1,0:T(8,128)(2,1)} collective-permute-done((bf16[8,128,512]{2,1,0:T(8,128)(2,1)S(1)}, bf16[8,128,512]{2,1,0:T(8,128)(2,1)}, u32[]{:S(2)}, u32[]{:S(2)}) %collective-permute-start.16) | collective-permute-done | bytes 1048608 | tf_op jit(solution)/shard_map/ppermute | solution.py:389
  94.1 4.6 %weight_part.1 = bf16[16,32,512]{2,1,0:T(8,128)(2,1)} custom-call(s32[5]{0:T(128)} %stack.23.place_ref, bf16[128,512]{1,0:T(8,128)(2,1)} %get-tuple-element.86.refs_0_, bf16[128,512]{1,0:T(8,128)(2,1)} %copy-done.13, bf16[128,512]{1,0:T(8,128)(2,1)} %copy-done.14, bf16[128,512]{1,0:T(8,128)(2,1)} %copy-done.15, bf16[128,512]{1,0:T(8,128)(2,1)} %copy-done.16, ...), custom_call_target="tpu_custom_call" | custom-call | tf_op jit(solution)/shard_map/weight_part/pallas_call | solution.py:263
  99.6 8.7 %all-to-all-start.2 = ((bf16[16,32,512]{2,1,0:T(8,128)(2,1)}), bf16[16,32,512]{2,1,0:T(8,128)(2,1)S(1)}, u32[]{:S(2)}, u32[]{:S(2)}) async-start(bf16[16,32,512]{2,1,0:T(8,128)(2,1)} %weight_part.1), calls=%async_computation.2 | async-start | bytes 1048576 | tf_op jit(solution)/shard_map/all_to_all | solution.py:392
  109.9 5.8 %collective-permute-done.17.refs_4_ = bf16[1024,256]{1,0:T(8,128)(2,1)S(1)} collective-permute-done((bf16[1024,256]{1,0:T(8,128)(2,1)}, bf16[1024,256]{1,0:T(8,128)(2,1)S(1)}, u32[]{:S(2)}, u32[]{:S(2)}) %collective-permute-start.17) | collective-permute-done | bytes 524320 | tf_op jit(solution)/shard_map/ppermute | solution.py:394
  115.7 1.5 collective-permute-start.22
  117.3 1.6 %collective-permute-done.22.refs_12_ = bf16[1024,256]{1,0:T(8,128)(2,1)} collective-permute-done((bf16[1024,256]{1,0:T(8,128)(2,1)S(1)}, bf16[1024,256]{1,0:T(8,128)(2,1)}, u32[]{:S(2)}, u32[]{:S(2)}) %collective-permute-start.22) | collective-permute-done | bytes 524320 | tf_op jit(solution)/shard_map/ppermute | solution.py:396
  118.9 6.2 %values.1.v_ref = bf16[16,32,128]{2,1,0:T(8,128)(2,1)} custom-call(s32[5]{0:T(128)} %stack.23.place_ref, s32[1,128]{1,0:T(1,128)} %order_ref.5, bf16[128,8192]{1,0:T(8,128)(2,1)} %x_ref.3, bf16[1024,256]{1,0:T(8,128)(2,1)} %copy-done.4, bf16[1024,256]{1,0:T(8,128)(2,1)} %collective-permute-done.5.refs_1_, bf16[1024,256]{1,0:T(8,128)(2,1)} %copy-done.7, ...), custom_call_target="tpu_custom_call" | custom-call | tf_op jit(solution)/shard_map/values/pallas_call | solution.py:323
  126.7 2.0 %share.1 = bf16[16,32,640]{2,1,0:T(8,128)(2,1)} custom-call(bf16[16,32,512]{2,1,0:T(8,128)(2,1)} %copy-done.5, bf16[16,32,128]{2,1,0:T(8,128)(2,1)} %values.1.v_ref), custom_call_target="tpu_custom_call" | custom-call | tf_op jit(solution)/shard_map/share/pallas_call | solution.py:345
  128.7 6.5 %all-to-all-start.3 = ((bf16[16,32,640]{2,1,0:T(8,128)(2,1)}), bf16[16,32,640]{2,1,0:T(8,128)(2,1)S(1)}, u32[]{:S(2)}, u32[]{:S(2)}) async-start(bf16[16,32,640]{2,1,0:T(8,128)(2,1)} %share.1), calls=%async_computation.3 | async-start | bytes 1310720 | tf_op jit(solution)/shard_map/all_to_all | solution.py:404
  135.2 7.6 %input_grad.1 = bf16[128,8192]{1,0:T(8,128)(2,1)} custom-call(s32[5]{0:T(128)} %stack.23.place_ref, bf16[128,512]{1,0:T(8,128)(2,1)} %get-tuple-element.102.grad_ref, bf16[1024,256]{1,0:T(8,128)(2,1)} %copy-done.4, bf16[1024,256]{1,0:T(8,128)(2,1)} %collective-permute-done.5.refs_1_, bf16[1024,256]{1,0:T(8,128)(2,1)} %copy-done.7, ...), custom_call_target="tpu_custom_call" | custom-call | tf_op jit(solution)/shard_map/input_grad/pallas_call | solution.py:323
  142.7 3.4 %all-to-all-done.3.v_ref.share_ref = bf16[16,32,640]{2,1,0:T(8,128)(2,1)S(1)} async-done(((bf16[16,32,640]{2,1,0:T(8,128)(2,1)}), bf16[16,32,640]{2,1,0:T(8,128)(2,1)S(1)}, u32[]{:S(2)}, u32[]{:S(2)}) %all-to-all-start.3) | async-done | bytes 655392 | tf_op jit(solution)/shard_map/all_to_all | solution.py:404
  147.0 9.4 %attend.1 = (bf16[128,4096]{1,0:T(8,128)(2,1)}, bf16[128,4096]{1,0:T(8,128)(2,1)}, bf16[128,512]{1,0:T(8,128)(2,1)}, f32[512,512]{1,0:T(8,128)}) custom-call(f32[128,4096]{1,0:T(8,128)} %get-tuple-element.76.probs_ref, bf16[128,4608]{1,0:T(8,128)(2,1)} %bitcast.9, bf16[128,4608]{1,0:T(8,128)(2,1)} %bitcast.10, bf16[16,32,640]{2,1,0:T(8,128)(2,1)} %copy-done.3, ...), custom_call_target="tpu_custom_call" | custom-call | tf_op jit(solution)/shard_map/attend/pallas_call | solution.py:212
  (87 shorter events, 13.1 us)
Async XLA Ops:
  0.6 27.1 %collective-permute-start.6 = (bf16[128,8192]{1,0:T(8,128)(2,1)}, bf16[128,8192]{1,0:T(8,128)(2,1)}, u32[]{:S(2)}, u32[]{:S(2)}) collective-permute-start(bf16[128,8192]{1,0:T(8,128)(2,1)} %x_ref.3), channel_id=1, source_target_pairs={{0,16},{16,0},{1,17},{17,1},{2,18},{18,2},{3,19},{19,3},{4,20},{20... | collective-permute-start | bytes 6291464 | tf_op jit(solution)/shard_map/ppermute | solution.py:362
  4.0 10.8 %collective-permute-start = (bf16[512,256]{1,0:T(8,128)(2,1)S(1)}, bf16[512,256]{1,0:T(8,128)(2,1)S(1)}, u32[]{:S(2)}, u32[]{:S(2)}) collective-permute-start(bf16[512,256]{1,0:T(8,128)(2,1)S(1)} %constant_dynamic-slice_fusion), channel_id=1, source_target_pairs={{0,1},{1,0},{2,3},{3,2},{4,5},{5,4},{6,7},{7,6},{8,9},{9,8},{10,11... | collective-permute-start | bytes 786440 | tf_op jit(solution)/shard_map/ppermute | solution.py:361
  5.5 9.2 %collective-permute-start.1 = (s32[1,128]{1,0:T(1,128)}, s32[1,128]{1,0:T(1,128)S(1)}, u32[]{:S(2)}, u32[]{:S(2)}) collective-permute-start(s32[1,128]{1,0:T(1,128)} %order_ref.5), channel_id=1, source_target_pairs={{0,16},{16,0},{1,17},{17,1},{2,18},{18,2},{3,19},{19,3},{4,20},{20... | collective-permute-start | bytes 1544 | tf_op jit(solution)/shard_map/ppermute | solution.py:363
  14.8 28.7 %all-to-all-start = ((bf16[16,8,4608]{2,1,0:T(8,128)(2,1)}), bf16[16,8,4608]{2,1,0:T(8,128)(2,1)S(1)}, u32[]{:S(2)}, u32[]{:S(2)}) async-start(bf16[16,8,4608]{2,1,0:T(8,128)(2,1)} %bitcast.11), calls=%async_computation | async-start | bytes 2359296 | tf_op jit(solution)/shard_map/all_to_all | solution.py:367
  19.4 72.3 %copy-start.4 = (bf16[1024,256]{1,0:T(8,128)(2,1)}, bf16[1024,256]{1,0:T(8,128)(2,1)S(1)}, u32[]{:S(2)}) copy-start(bf16[1024,256]{1,0:T(8,128)(2,1)S(1)} %pad_maximum_fusion.refs_0_) | copy-start | bytes 1572868
  19.4 21.4 %collective-permute-start.4 = (bf16[1024,256]{1,0:T(8,128)(2,1)S(1)}, bf16[1024,256]{1,0:T(8,128)(2,1)}, u32[]{:S(2)}, u32[]{:S(2)}) collective-permute-start(bf16[1024,256]{1,0:T(8,128)(2,1)S(1)} %pad_maximum_fusion.refs_0_), channel_id=1, source_target_pairs={{0,2},{2,4},{4,6},{6,8},{8,10},{10,12},{12,14},{14,0},{1,3},{3,5},... | collective-permute-start | bytes 1572872 | tf_op jit(solution)/shard_map/ppermute | solution.py:375
  21.1 22.1 %collective-permute-start.5 = (bf16[1024,256]{1,0:T(8,128)(2,1)S(1)}, bf16[1024,256]{1,0:T(8,128)(2,1)}, u32[]{:S(2)}, u32[]{:S(2)}) collective-permute-start(bf16[1024,256]{1,0:T(8,128)(2,1)S(1)} %pad_maximum_fusion.refs_0_), channel_id=1, source_target_pairs={{0,14},{2,0},{4,2},{6,4},{8,6},{10,8},{12,10},{14,12},{1,15},{3,1}... | collective-permute-start | bytes 1572872 | tf_op jit(solution)/shard_map/ppermute | solution.py:376
  25.2 12.6 %collective-permute-start.2 = (bf16[128,512]{1,0:T(8,128)(2,1)}, bf16[128,512]{1,0:T(8,128)(2,1)S(1)}, u32[]{:S(2)}, u32[]{:S(2)}) collective-permute-start(bf16[128,512]{1,0:T(8,128)(2,1)} %get-tuple-element.67), channel_id=1, source_target_pairs={{0,32},{32,0},{64,96},{96,64},{128,160},{160,128},{192,224},{224,1... | collective-permute-start | bytes 393224 | tf_op jit(solution)/shard_map/ppermute | solution.py:374
  26.5 13.4 %collective-permute-start.3 = (bf16[128,512]{1,0:T(8,128)(2,1)}, bf16[128,512]{1,0:T(8,128)(2,1)S(1)}, u32[]{:S(2)}, u32[]{:S(2)}) collective-permute-start(bf16[128,512]{1,0:T(8,128)(2,1)} %get-tuple-element.68), channel_id=1, source_target_pairs={{0,64},{32,96},{64,0},{96,32},{128,192},{160,224},{192,128},{224,1... | collective-permute-start | bytes 393224 | tf_op jit(solution)/shard_map/ppermute | solution.py:374
  27.7 22.0 %collective-permute-start.7 = (bf16[128,512]{1,0:T(8,128)(2,1)}, bf16[128,512]{1,0:T(8,128)(2,1)S(1)}, u32[]{:S(2)}, u32[]{:S(2)}) collective-permute-start(bf16[128,512]{1,0:T(8,128)(2,1)} %get-tuple-element.81), channel_id=1, source_target_pairs={{0,96},{32,64},{64,32},{96,0},{128,224},{160,192},{192,160},{224,1... | collective-permute-start | bytes 393224 | tf_op jit(solution)/shard_map/ppermute | solution.py:374
  37.8 56.4 %copy-start.13 = (bf16[128,512]{1,0:T(8,128)(2,1)}, bf16[128,512]{1,0:T(8,128)(2,1)S(1)}, u32[]{:S(2)}) copy-start(bf16[128,512]{1,0:T(8,128)(2,1)S(1)} %collective-permute-done.2.refs_1_) | copy-start | bytes 393220
  37.8 12.0 %collective-permute-start.8 = (bf16[128,512]{1,0:T(8,128)(2,1)}, bf16[128,512]{1,0:T(8,128)(2,1)S(1)}, u32[]{:S(2)}, u32[]{:S(2)}) collective-permute-start(bf16[128,512]{1,0:T(8,128)(2,1)} %get-tuple-element.82), channel_id=1, source_target_pairs={{0,128},{32,160},{64,192},{96,224},{128,0},{160,32},{192,64},{224,... | collective-permute-start | bytes 393224 | tf_op jit(solution)/shard_map/ppermute | solution.py:374
  39.9 9.8 %collective-permute-start.10 = (bf16[128,512]{1,0:T(8,128)(2,1)}, bf16[128,512]{1,0:T(8,128)(2,1)S(1)}, u32[]{:S(2)}, u32[]{:S(2)}) collective-permute-start(bf16[128,512]{1,0:T(8,128)(2,1)} %get-tuple-element.84), channel_id=1, source_target_pairs={{0,192},{32,224},{64,128},{96,160},{128,64},{160,96},{192,0},{224,... | collective-permute-start | bytes 393224 | tf_op jit(solution)/shard_map/ppermute | solution.py:374
  40.8 13.6 %collective-permute-start.11 = (bf16[128,512]{1,0:T(8,128)(2,1)S(1)}, bf16[128,512]{1,0:T(8,128)(2,1)S(1)}, u32[]{:S(2)}, u32[]{:S(2)}) collective-permute-start(bf16[128,512]{1,0:T(8,128)(2,1)S(1)} %copy-done.22), channel_id=1, source_target_pairs={{0,224},{32,192},{64,160},{96,128},{128,96},{160,64},{192,32},{224... | collective-permute-start | bytes 393224 | tf_op jit(solution)/shard_map/ppermute | solution.py:374
  43.2 11.2 %collective-permute-start.9 = (bf16[128,512]{1,0:T(8,128)(2,1)S(1)}, bf16[128,512]{1,0:T(8,128)(2,1)S(1)}, u32[]{:S(2)}, u32[]{:S(2)}) collective-permute-start(bf16[128,512]{1,0:T(8,128)(2,1)S(1)} %copy-done.21), channel_id=1, source_target_pairs={{0,160},{32,128},{64,224},{96,192},{128,32},{160,0},{192,96},{224,... | collective-permute-start | bytes 393224 | tf_op jit(solution)/shard_map/ppermute | solution.py:374
  55.1 34.5 %all-to-all-start.1 = ((bf16[8,256,512]{2,1,0:T(8,128)(2,1)}), bf16[8,256,512]{2,1,0:T(8,128)(2,1)S(1)}, u32[]{:S(2)}, u32[]{:S(2)}) async-start(bf16[8,256,512]{2,1,0:T(8,128)(2,1)} %get-tuple-element.94), calls=%async_computation.1 | async-start | bytes 4194304 | tf_op jit(solution)/shard_map/all_to_all | solution.py:385
  58.7 17.1 %collective-permute-start.12 = (bf16[1024,256]{1,0:T(8,128)(2,1)}, bf16[1024,256]{1,0:T(8,128)(2,1)S(1)}, u32[]{:S(2)}, u32[]{:S(2)}) collective-permute-start(bf16[1024,256]{1,0:T(8,128)(2,1)} %collective-permute-done.4.refs_7_), channel_id=1, source_target_pairs={{0,2},{2,4},{4,6},{6,8},{8,10},{10,12},{12,14},{14,0},{1,3},{3,5},... | collective-permute-start | bytes 1572872 | tf_op jit(solution)/shard_map/ppermute | solution.py:382
  60.1 15.7 %collective-permute-start.14 = (bf16[1024,256]{1,0:T(8,128)(2,1)}, bf16[1024,256]{1,0:T(8,128)(2,1)S(1)}, u32[]{:S(2)}, u32[]{:S(2)}) collective-permute-start(bf16[1024,256]{1,0:T(8,128)(2,1)} %collective-permute-done.5.refs_1_), channel_id=1, source_target_pairs={{0,14},{2,0},{4,2},{6,4},{8,6},{10,8},{12,10},{14,12},{1,15},{3,1}... | collective-permute-start | bytes 1572872 | tf_op jit(solution)/shard_map/ppermute | solution.py:383
  75.9 13.4 %collective-permute-start.13 = (bf16[1024,256]{1,0:T(8,128)(2,1)S(1)}, bf16[1024,256]{1,0:T(8,128)(2,1)}, u32[]{:S(2)}, u32[]{:S(2)}) collective-permute-start(bf16[1024,256]{1,0:T(8,128)(2,1)S(1)} %collective-permute-done.12.refs_6_), channel_id=1, source_target_pairs={{0,2},{2,4},{4,6},{6,8},{8,10},{10,12},{12,14},{14,0},{1,3},{3,5},... | collective-permute-start | bytes 1572872 | tf_op jit(solution)/shard_map/ppermute | solution.py:386
  75.9 13.4 %collective-permute-start.15 = (bf16[1024,256]{1,0:T(8,128)(2,1)S(1)}, bf16[1024,256]{1,0:T(8,128)(2,1)}, u32[]{:S(2)}, u32[]{:S(2)}) collective-permute-start(bf16[1024,256]{1,0:T(8,128)(2,1)S(1)} %collective-permute-done.14.refs_2_), channel_id=1, source_target_pairs={{0,14},{2,0},{4,2},{6,4},{8,6},{10,8},{12,10},{14,12},{1,15},{3,1}... | collective-permute-start | bytes 1572872 | tf_op jit(solution)/shard_map/ppermute | solution.py:387
  89.7 4.5 %collective-permute-start.16 = (bf16[8,128,512]{2,1,0:T(8,128)(2,1)S(1)}, bf16[8,128,512]{2,1,0:T(8,128)(2,1)}, u32[]{:S(2)}, u32[]{:S(2)}) collective-permute-start(bf16[8,128,512]{2,1,0:T(8,128)(2,1)S(1)} %slice.3), channel_id=1, source_target_pairs={{0,16},{16,0},{1,17},{17,1},{2,18},{18,2},{3,19},{19,3},{4,20},{20... | collective-permute-start | bytes 3145736 | tf_op jit(solution)/shard_map/ppermute | solution.py:389
  91.7 17.6 %collective-permute-start.18 = (bf16[1024,256]{1,0:T(8,128)(2,1)S(1)}, bf16[1024,256]{1,0:T(8,128)(2,1)}, u32[]{:S(2)}, u32[]{:S(2)}) collective-permute-start(bf16[1024,256]{1,0:T(8,128)(2,1)S(1)} %pad_maximum_fusion.refs_0_), channel_id=1, source_target_pairs={{0,16},{16,0},{1,17},{17,1},{2,18},{18,2},{3,19},{19,3},{4,20},{20... | collective-permute-start | bytes 1572872 | tf_op jit(solution)/shard_map/ppermute | solution.py:396
  91.8 17.6 %collective-permute-start.19 = (bf16[1024,256]{1,0:T(8,128)(2,1)}, bf16[1024,256]{1,0:T(8,128)(2,1)}, u32[]{:S(2)}, u32[]{:S(2)}) collective-permute-start(bf16[1024,256]{1,0:T(8,128)(2,1)} %collective-permute-done.5.refs_1_), channel_id=1, source_target_pairs={{0,16},{16,0},{1,17},{17,1},{2,18},{18,2},{3,19},{19,3},{4,20},{20... | collective-permute-start | bytes 1572872 | tf_op jit(solution)/shard_map/ppermute | solution.py:396
  92.2 17.6 %collective-permute-start.25 = (bf16[1024,256]{1,0:T(8,128)(2,1)}, bf16[1024,256]{1,0:T(8,128)(2,1)}, u32[]{:S(2)}, u32[]{:S(2)}) collective-permute-start(bf16[1024,256]{1,0:T(8,128)(2,1)} %collective-permute-done.4.refs_7_), channel_id=1, source_target_pairs={{0,16},{16,0},{1,17},{17,1},{2,18},{18,2},{3,19},{19,3},{4,20},{20... | collective-permute-start | bytes 1572872 | tf_op jit(solution)/shard_map/ppermute | solution.py:396
  98.8 16.9 %collective-permute-start.17 = (bf16[1024,256]{1,0:T(8,128)(2,1)}, bf16[1024,256]{1,0:T(8,128)(2,1)S(1)}, u32[]{:S(2)}, u32[]{:S(2)}) collective-permute-start(bf16[1024,256]{1,0:T(8,128)(2,1)} %collective-permute-done.13.refs_5_), channel_id=1, source_target_pairs={{0,2},{2,4},{4,6},{6,8},{8,10},{10,12},{12,14},{14,0},{1,3},{3,5},... | collective-permute-start | bytes 1572872 | tf_op jit(solution)/shard_map/ppermute | solution.py:394
  99.6 26.3 %all-to-all-start.2 = ((bf16[16,32,512]{2,1,0:T(8,128)(2,1)}), bf16[16,32,512]{2,1,0:T(8,128)(2,1)S(1)}, u32[]{:S(2)}, u32[]{:S(2)}) async-start(bf16[16,32,512]{2,1,0:T(8,128)(2,1)} %weight_part.1), calls=%async_computation.2 | async-start | bytes 1048576 | tf_op jit(solution)/shard_map/all_to_all | solution.py:392
  108.3 9.0 %collective-permute-start.20 = (bf16[1024,256]{1,0:T(8,128)(2,1)}, bf16[1024,256]{1,0:T(8,128)(2,1)S(1)}, u32[]{:S(2)}, u32[]{:S(2)}) collective-permute-start(bf16[1024,256]{1,0:T(8,128)(2,1)} %copy-done.7), channel_id=1, source_target_pairs={{0,16},{16,0},{1,17},{17,1},{2,18},{18,2},{3,19},{19,3},{4,20},{20... | collective-permute-start | bytes 1572872 | tf_op jit(solution)/shard_map/ppermute | solution.py:396
  109.3 7.9 %collective-permute-start.24 = (bf16[1024,256]{1,0:T(8,128)(2,1)}, bf16[1024,256]{1,0:T(8,128)(2,1)S(1)}, u32[]{:S(2)}, u32[]{:S(2)}) collective-permute-start(bf16[1024,256]{1,0:T(8,128)(2,1)} %copy-done.6), channel_id=1, source_target_pairs={{0,16},{16,0},{1,17},{17,1},{2,18},{18,2},{3,19},{19,3},{4,20},{20... | collective-permute-start | bytes 1572872 | tf_op jit(solution)/shard_map/ppermute | solution.py:396
  109.4 7.8 %collective-permute-start.21 = (bf16[1024,256]{1,0:T(8,128)(2,1)}, bf16[1024,256]{1,0:T(8,128)(2,1)S(1)}, u32[]{:S(2)}, u32[]{:S(2)}) collective-permute-start(bf16[1024,256]{1,0:T(8,128)(2,1)} %collective-permute-done.15.refs_3_), channel_id=1, source_target_pairs={{0,16},{16,0},{1,17},{17,1},{2,18},{18,2},{3,19},{19,3},{4,20},{20... | collective-permute-start | bytes 1572872 | tf_op jit(solution)/shard_map/ppermute | solution.py:396
  109.8 7.4 %collective-permute-start.23 = (bf16[1024,256]{1,0:T(8,128)(2,1)}, bf16[1024,256]{1,0:T(8,128)(2,1)S(1)}, u32[]{:S(2)}, u32[]{:S(2)}) collective-permute-start(bf16[1024,256]{1,0:T(8,128)(2,1)} %collective-permute-done.13.refs_5_), channel_id=1, source_target_pairs={{0,16},{16,0},{1,17},{17,1},{2,18},{18,2},{3,19},{19,3},{4,20},{20... | collective-permute-start | bytes 1572872 | tf_op jit(solution)/shard_map/ppermute | solution.py:396
  115.7 3.2 %collective-permute-start.22 = (bf16[1024,256]{1,0:T(8,128)(2,1)S(1)}, bf16[1024,256]{1,0:T(8,128)(2,1)}, u32[]{:S(2)}, u32[]{:S(2)}) collective-permute-start(bf16[1024,256]{1,0:T(8,128)(2,1)S(1)} %collective-permute-done.17.refs_4_), channel_id=1, source_target_pairs={{0,16},{16,0},{1,17},{17,1},{2,18},{18,2},{3,19},{19,3},{4,20},{20... | collective-permute-start | bytes 1572872 | tf_op jit(solution)/shard_map/ppermute | solution.py:396
  128.7 17.4 %all-to-all-start.3 = ((bf16[16,32,640]{2,1,0:T(8,128)(2,1)}), bf16[16,32,640]{2,1,0:T(8,128)(2,1)S(1)}, u32[]{:S(2)}, u32[]{:S(2)}) async-start(bf16[16,32,640]{2,1,0:T(8,128)(2,1)} %share.1), calls=%async_computation.3 | async-start | bytes 1310720 | tf_op jit(solution)/shard_map/all_to_all | solution.py:404
  (21 other events, 175.8 us)

commit v2 on v1

--- a/solution.py
+++ b/solution.py
@@ -83,75 +83,68 @@
             put(t * 2 + u, dealt[:, u * HD : (u + 1) * HD])
 
 
-def sort_own_kernel(place_ref, order_ref, x_ref, *refs):
-    *out_refs, deal_ref, rows_ref, dealt_ref = refs
-    here = place_ref[0] * 2 + place_ref[1]
-
-    def put(n, block):
-        dealt_ref[here ^ n] = block
-
-    deal_columns(place_ref, order_ref, x_ref, deal_ref, rows_ref, put)
-    for k in range(PEERS):
-        out_refs[k][...] = dealt_ref[k]
-
-
-def sort_other_kernel(place_ref, order_ref, x_ref, out_ref, deal_ref, rows_ref):
+def sort_own_kernel(place_ref, order_ref, x_ref, out_ref, deal_ref, rows_ref):
     def put(n, block):
         out_ref[n] = block
 
     deal_columns(place_ref, order_ref, x_ref, deal_ref, rows_ref, put)
 
 
-def sort_x(place, order, x, own):
-    scratch = [pltpu.VMEM((DEAL, 2 * HD), jnp.bfloat16), pltpu.VMEM((ROWS, 4 * KVW), jnp.bfloat16)]
-    if own:
-        out_specs = [pl.BlockSpec((ROWS, HD), lambda i: (0, i))] * PEERS
-        out_shape = [jax.ShapeDtypeStruct((ROWS, KVW), jnp.bfloat16)] * PEERS
-        scratch.append(pltpu.VMEM((PEERS, ROWS, HD), jnp.bfloat16))
-    else:
-        out_specs = pl.BlockSpec((PEERS, ROWS, HD), lambda i: (0, 1, i))
-        out_shape = jax.ShapeDtypeStruct((PEERS, 2 * ROWS, KVW), jnp.bfloat16)
+def sort_other_kernel(place_ref, order_ref, x_ref, _, out_ref, deal_ref, rows_ref):
+    sort_own_kernel(place_ref, order_ref, x_ref, out_ref, deal_ref, rows_ref)
+
+
+def sort_x(place, order, x, payload=None):
+    own = payload is None
+    in_specs = [
+        pl.BlockSpec(memory_space=pltpu.SMEM),
+        pl.BlockSpec((1, ROWS), lambda i: (0, 0)),
+        pl.BlockSpec((ROWS, 4 * KVW), lambda i: (0, i)),
+    ]
+    operands = [place, order, x]
+    if not own:
+        in_specs.append(pl.BlockSpec(memory_space=pl.ANY))
+        operands.append(payload)
     return pl.pallas_call(
         sort_own_kernel if own else sort_other_kernel,
         grid=(4,),
-        in_specs=[
-            pl.BlockSpec(memory_space=pltpu.SMEM),
-            pl.BlockSpec((1, ROWS), lambda i: (0, 0)),
-            pl.BlockSpec((ROWS, 4 * KVW), lambda i: (0, i)),
-        ],
-        out_specs=out_specs,
-        out_shape=out_shape,
-        scratch_shapes=scratch,
+        in_specs=in_specs,
+        out_specs=pl.BlockSpec((PEERS, ROWS, HD), lambda i: (0, 0 if own else 1, i)),
+        out_shape=jax.ShapeDtypeStruct((PEERS, ROWS if own else 2 * ROWS, KVW), jnp.bfloat16),
+        scratch_shapes=[
+            pltpu.VMEM((DEAL, 2 * HD), jnp.bfloat16),
+            pltpu.VMEM((ROWS, 4 * KVW), jnp.bfloat16),
+        ],
+        input_output_aliases={} if own else {3: 0},
         cost_estimate=LIGHT,
         compiler_params=pltpu.CompilerParams(vmem_limit_bytes=VMEM),
         name="sort_own" if own else "sort_other",
-    )(place, order, x)
-
-
-def probs_kernel(seg_ref, q_ref, k_ref, grad_ref, _, probs_ref, value_grad_ref, payload_ref):
+    )(*operands)
+
+
+def stack_heads(ref):
+    return jnp.concatenate([ref[:, r * HD : (r + 1) * HD] for r in range(GROUP)], axis=0)
+
+
+def probs_kernel(seg_ref, q_ref, k_ref, grad_ref, probs_ref, value_grad_ref, payload_ref):
     seg_query = jnp.broadcast_to(seg_ref[...], (ROWS, ROWS))
     seg_key = seg_query.T
     key_at = lax.broadcasted_iota(jnp.int32, (ROWS, ROWS), 0)
     query_at = lax.broadcasted_iota(jnp.int32, (ROWS, ROWS), 1)
-    allowed = (seg_key == seg_query) & (key_at <= query_at)
-    bias = jnp.where(allowed, 0.0, -1e30).astype(jnp.float32)
-    total = jnp.zeros((ROWS, HD), jnp.float32)
-    for r in range(GROUP):
-        head = slice(r * HD, (r + 1) * HD)
-        scores = dot(k_ref[...], q_ref[:, head], NT) * FACTOR
-        scores = jnp.where(allowed, scores, bias)
-        highest = jnp.max(scores, axis=0, keepdims=True)
-        expon = jnp.exp(scores - highest)
-        probs = expon / jnp.sum(expon, axis=0, keepdims=True)
-        probs_ref[:, head] = probs
-        total += dot(probs.astype(jnp.bfloat16), grad_ref[:, head])
-    total = total.astype(jnp.bfloat16)
+    allowed = ((seg_key == seg_query) & (key_at <= query_at)).astype(jnp.float32)
+    allowed = jnp.concatenate([allowed] * GROUP, axis=1) > 0
+    scores = dot(k_ref[...], stack_heads(q_ref), NT) * FACTOR
+    scores = jnp.where(allowed, scores, -1e30)
+    expon = jnp.exp(scores - jnp.max(scores, axis=0, keepdims=True))
+    probs = expon * (1.0 / jnp.sum(expon, axis=0, keepdims=True))
+    probs_ref[...] = probs
+    total = dot(probs.astype(jnp.bfloat16), stack_heads(grad_ref)).astype(jnp.bfloat16)
     value_grad_ref[...] = total
     for n in range(PEERS):
         payload_ref[n] = total
 
 
-def make_probs(seg, moved, out_grad, payload):
+def make_probs(seg, moved, out_grad):
     wide = GROUP * HD
     return pl.pallas_call(
         probs_kernel,
@@ -161,7 +154,6 @@
             pl.BlockSpec((ROWS, wide), lambda i: (0, i)),
             pl.BlockSpec((ROWS, HD), lambda i: (0, HEADS + i)),
             pl.BlockSpec((ROWS, wide), lambda i: (0, i)),
-            pl.BlockSpec(memory_space=pl.ANY),
         ],
         out_specs=[
             pl.BlockSpec((ROWS, wide), lambda i: (0, i)),
@@ -171,13 +163,12 @@
         out_shape=[
             jax.ShapeDtypeStruct((ROWS, HQW), jnp.float32),
             jax.ShapeDtypeStruct((ROWS, KVW), jnp.bfloat16),
-            jax.ShapeDtypeStruct(payload.shape, payload.dtype),
-        ],
-        input_output_aliases={4: 2},
+            jax.ShapeDtypeStruct((PEERS, 2 * ROWS, KVW), jnp.bfloat16),
+        ],
         cost_estimate=LIGHT,
         compiler_params=pltpu.CompilerParams(vmem_limit_bytes=VMEM),
         name="probs",
-    )(seg, moved, moved, out_grad, payload)
+    )(seg, moved, moved, out_grad)
 
 
 def attend_kernel(probs_ref, q_ref, k_ref, v_ref, share_ref, grad_ref, *refs):
@@ -191,18 +182,19 @@
     each = ROWS // N_DP
     own = pl.ds(pl.multiple_of(pl.program_id(0) * each, each), each)
     value = jnp.concatenate([wide_ref[source, own, :] for source in range(N_DP)], axis=0).astype(jnp.bfloat16)
-    total = jnp.zeros((ROWS, HD), jnp.float32)
+    grads, queries = stack_heads(grad_ref), stack_heads(q_ref)
+    probs = probs_ref[...]
+    probs_b = probs.astype(jnp.bfloat16)
+    attended = dot(probs_b, value, TN).astype(jnp.bfloat16)
+    dprob = dot(value, grads, NT)
+    delta = jnp.sum(probs_b.astype(jnp.float32) * dprob, axis=0, keepdims=True)
+    dscore = (probs * (dprob - delta)).astype(jnp.bfloat16)
+    query_grad = (dot(dscore, k_ref[...], TN) * FACTOR).astype(jnp.bfloat16)
     for r in range(GROUP):
         head = slice(r * HD, (r + 1) * HD)
-        probs = probs_ref[:, head]
-        probs_b = probs.astype(jnp.bfloat16)
-        attended_ref[:, head] = dot(probs_b, value, TN).astype(jnp.bfloat16)
-        dprob = dot(value, grad_ref[:, head], NT)
-        delta = jnp.sum(probs_b.astype(jnp.float32) * dprob, axis=0, keepdims=True)
-        dscore = (probs * (dprob - delta)).astype(jnp.bfloat16)
-        query_grad_ref[:, head] = (dot(dscore, k_ref[...], TN) * FACTOR).astype(jnp.bfloat16)
-        total += dot(dscore, q_ref[:, head])
-    key_grad_ref[...] = (total * FACTOR).astype(jnp.bfloat16)
+        attended_ref[:, head] = attended[head]
+        query_grad_ref[:, head] = query_grad[head]
+    key_grad_ref[...] = (dot(dscore, queries) * FACTOR).astype(jnp.bfloat16)
 
 
 def attend(probs, moved, got, out_grad):
@@ -234,12 +226,10 @@
     )(probs, moved, moved, got, got, out_grad)
 
 
-def weight_kernel(place_ref, *refs):
-    x_refs, both_ref, other_ref, out_ref, wide_ref, total_ref = refs[:PEERS], *refs[PEERS:]
+def weight_kernel(place_ref, own_ref, both_ref, other_ref, out_ref, wide_ref, total_ref):
     core = place_ref[2]
-    here = place_ref[0] * 2 + place_ref[1]
     for k in range(PEERS):
-        wide_ref[(here ^ k) * 2 + core] = x_refs[k][...].astype(jnp.float32)
+        wide_ref[k * 2 + core] = own_ref[k].astype(jnp.float32)
         wide_ref[k * 2 + 1 - core] = both_ref[k, ROWS:, :].astype(jnp.float32)
     for step in range(PEERS // 2):
         lhs, rhs = [], []
@@ -258,11 +248,11 @@
             out_ref[...] = (total_ref[...] + part).astype(jnp.bfloat16).reshape(out_ref.shape)
 
 
-def weight_part(place, rows_x, both, other):
+def weight_part(place, own, both, other):
     vmem = pl.BlockSpec(memory_space=pltpu.VMEM)
     return pl.pallas_call(
         weight_kernel,
-        in_specs=[pl.BlockSpec(memory_space=pltpu.SMEM)] + [vmem] * (PEERS + 2),
+        in_specs=[pl.BlockSpec(memory_space=pltpu.SMEM)] + [vmem] * 3,
         out_specs=vmem,
         out_shape=jax.ShapeDtypeStruct((N_SHARD, SUB, KVW), jnp.bfloat16),
         scratch_shapes=[
@@ -272,7 +262,7 @@
         cost_estimate=LIGHT,
         compiler_params=pltpu.CompilerParams(vmem_limit_bytes=VMEM),
         name="weight_part",
-    )(place, *rows_x, both, other)
+    )(place, own, both, other)
 
 
 def column_blocks(place_ref):
@@ -362,36 +352,33 @@
     other_x = lax.ppermute(layer_input, "c", swap(2, 1))
     other_order = lax.ppermute(send_order, "c", swap(2, 1))
     sent = sort_qk(send_order, queries, key_rows)
-    rows_x = list(sort_x(place, send_order, layer_input, True))
-    other, other_order, sent, rows_x = lax.optimization_barrier((other, other_order, sent, rows_x))
+    own_x = sort_x(place, send_order, layer_input)
+    other, other_order, sent = lax.optimization_barrier((other, other_order, sent))
     moved = lax.all_to_all(
         sent.reshape(N_DP, ROWS // N_DP, HQW + KVW), DP, split_axis=0, concat_axis=0, tiled=True
     ).reshape(ROWS, HQW + KVW)
     weight = jnp.concatenate([half, other], axis=0)
     up, down = [weight], [weight]
-    payload = sort_x(place, other_order, other_x, False)
-    payload, rows_x[5:] = lax.optimization_barrier((payload, rows_x[5:]))
-    rows_x = rows_x[:1] + [lax.ppermute(rows_x[k], peers, swap(PEERS, k)) for k in range(1, PEERS)]
     up.append(lax.ppermute(up[0], "z", right))
     down.append(lax.ppermute(down[0], "z", left))
-
-    early = 3
-    moved, rows_x[:early], up[1], down[1] = lax.optimization_barrier((moved, rows_x[:early], up[1], down[1]))
-    probs, value_grad, payload = make_probs(segment_ids, moved, out_grad, payload)
-
+    moved, up[1], down[1], own_x = lax.optimization_barrier((moved, up[1], down[1], own_x))
+    own_rows = lax.all_to_all(own_x, peers, split_axis=0, concat_axis=0, tiled=True)
     up.append(lax.ppermute(up[1], "z", right))
     down.append(lax.ppermute(down[1], "z", left))
-    payload, rows_x = lax.optimization_barrier((payload, rows_x))
+    probs, value_grad, payload = make_probs(segment_ids, moved, out_grad)
+    payload = sort_x(place, other_order, other_x, payload)
+
+    payload, own_rows, up, down = lax.optimization_barrier((payload, own_rows, up, down))
     both = lax.all_to_all(payload, peers, split_axis=0, concat_axis=0, tiled=True)
     up.append(lax.ppermute(up[2], "z", right))
     down.append(lax.ppermute(down[2], "z", left))
-    both, up[3], down[3] = lax.optimization_barrier((both, up[3], down[3]))
+    up.append(lax.ppermute(up[3], "z", right))
+    both, up, down = lax.optimization_barrier((both, up, down))
     other_grads = lax.ppermute(both[:, :ROWS], "c", swap(2, 1))
-    partial = weight_part(place, rows_x, both, other_grads)
-    partial, up[3] = lax.optimization_barrier((partial, up[3]))
+    partial = weight_part(place, own_rows, both, other_grads)
+    partial, up, down = lax.optimization_barrier((partial, up, down))
     shares = lax.all_to_all(partial, SHARD, split_axis=0, concat_axis=0, tiled=True)
 
-    up.append(lax.ppermute(up[3], "z", right))
     own = down[:4] + up[4:0:-1]
     other = [lax.ppermute(one, "c", swap(2, 1)) for one in own]
     sent_v = with_weight(

time: 157 us -> 153 us (0.975)
  starting transfers between devices: 57.9 us -> 52.5 us
  Pallas kernels: 47.6 us -> 42.7 us
  waiting for transfers between devices: 45.9 us -> 50.4 us
  local copies, waits for them, and re-layouts: 4.11 us -> 5.77 us
    ppermute x1, waiting for transfers between devices: 11.7 us -> 1.88 us  [per_device(): up.append(lax.ppermute(up[1], 'z', right))]
    ppermute x7 -> x0, waiting for transfers between devices: 9.74 us -> none  [per_device(): lax.ppermute(rows_x[k], peers, swap(PEERS, k))]
    ppermute x7 -> x0, starting transfers between devices: 8.34 us -> none  [per_device(): lax.ppermute(rows_x[k], peers, swap(PEERS, k))]
    ppermute x1, waiting for transfers between devices: 0.01 us -> 6.63 us  [per_device(): up.append(lax.ppermute(up[0], 'z', right))]
    all_to_all x1, waiting for transfers between devices: 0.77 us -> 6.08 us  [per_device(): lax.all_to_all(partial, SHARD, split_axis=0, concat_axis=0, tiled=True)]
    all_to_all x0 -> x1, starting transfers between devices: none -> 4.89 us  [per_device(): lax.all_to_all(own_x, peers, split_axis=0, concat_axis=0, tiled=True)]
    ppermute x1, waiting for transfers between devices: 5.81 us -> 10.2 us  [per_device(): up.append(lax.ppermute(up[3], 'z', right))]
    all_to_all x1, waiting for transfers between devices: 0.28 us -> 4.57 us  [per_device(): lax.all_to_all(payload, peers, split_axis=0, concat_axis=0, tiled=True)]
  transfers between devices with their start and end apart: 30 -> 24, of which waited for: 10 -> 14; matrix products, arithmetic and copies ran while one was open for 0% -> 0% of each run, Pallas kernels for 23% -> 20%
where the time goes in v2:
time: 153 us; the launch traced here: 152 us
  starting transfers between devices  52.5 us (34%)
  waiting for transfers between devices  50.4 us (33%)
  Pallas kernels  42.7 us (28%)
  local copies, waits for them, and re-layouts  5.77 us (4%)
    pallas_call x2, Pallas kernels, with_weight(): pl.pallas_call(kernel, in_specs=[pl.BlockSpec(memory_space=pltpu.SMEM)] +...  13.8 us
    ppermute x1, waiting for transfers between devices, per_device(): up.append(lax.ppermute(up[3], 'z', right))  10.2 us
    ppermute x1, waiting for transfers between devices, per_device(): up.append(lax.ppermute(up[2], 'z', right))  10.1 us
    pallas_call x2, Pallas kernels, sort_x(): pl.pallas_call(sort_own_kernel if own else sort_other_kernel, grid=(4,),...  9.74 us
    all_to_all x1, starting transfers between devices, per_device(): lax.all_to_all(sent.reshape(N_DP, ROWS // N_DP, HQW + KVW), DP, split_axi...  7.66 us
    all_to_all x1, starting transfers between devices, per_device(): lax.all_to_all(partial, SHARD, split_axis=0, concat_axis=0, tiled=True)  7.27 us
    ppermute x1, waiting for transfers between devices, per_device(): up.append(lax.ppermute(up[0], 'z', right))  6.63 us
    all_to_all x1, waiting for transfers between devices, per_device(): lax.all_to_all(partial, SHARD, split_axis=0, concat_axis=0, tiled=True)  6.08 us
  transfers between devices with their start and end apart: 24, of which 14 were waited for; matrix products, arithmetic and copies ran while one was open for 0% of the time, Pallas kernels for 20%

profile of v2, /device:TPU:1, one launch (start us, length us, event | category | flops | bytes accessed | tf_op | source)
XLA Modules:
  0.0 152.2 jit_solution(10740587730706515393)
XLA Ops:
  0.7 1.0 copy-done
  1.7 3.8 %collective-permute-start = (bf16[512,256]{1,0:T(8,128)(2,1)S(1)}, bf16[512,256]{1,0:T(8,128)(2,1)S(1)}, u32[]{:S(2)}, u32[]{:S(2)}) collective-permute-start(bf16[512,256]{1,0:T(8,128)(2,1)S(1)} %constant_dynamic-slice_fusion), channel_id=1, source_target_pairs={{0,1},{1,0},{2,3},{3,2},{4,5},{5,4},{6,7},{7,6},{8,9},{9,8},{10,11... | collective-permute-start | bytes 786440 | tf_op jit(solution)/shard_map/ppermute | solution.py:351
  5.5 1.0 collective-permute-start.4
  6.5 2.7 %sort_qk.1 = bf16[128,4608]{1,0:T(8,128)(2,1)} custom-call(s32[1,128]{1,0:T(1,128)} %order_ref.5, bf16[128,4096]{1,0:T(8,128)(2,1)} %q_ref.1, bf16[128,512]{1,0:T(8,128)(2,1)} %k_ref.1), custom_call_target="tpu_custom_call" | custom-call | tf_op jit(solution)/shard_map/sort_qk/pallas_call | solution.py:52
  9.2 1.0 collective-permute-done.1.order_ref
  10.5 7.7 %all-to-all-start = ((bf16[16,8,4608]{2,1,0:T(8,128)(2,1)}), bf16[16,8,4608]{2,1,0:T(8,128)(2,1)S(1)}, u32[]{:S(2)}, u32[]{:S(2)}) async-start(bf16[16,8,4608]{2,1,0:T(8,128)(2,1)} %bitcast.11), calls=%async_computation | async-start | bytes 2359296 | tf_op jit(solution)/shard_map/all_to_all | solution.py:357
  18.2 1.7 %collective-permute-start.2 = (bf16[1024,256]{1,0:T(8,128)(2,1)S(1)}, bf16[1024,256]{1,0:T(8,128)(2,1)S(1)}, u32[]{:S(2)}, u32[]{:S(2)}) collective-permute-start(bf16[1024,256]{1,0:T(8,128)(2,1)S(1)} %pad_maximum_fusion.refs_0_), channel_id=1, source_target_pairs={{0,2},{2,4},{4,6},{6,8},{8,10},{10,12},{12,14},{14,0},{1,3},{3,5},... | collective-permute-start | bytes 1572872 | tf_op jit(solution)/shard_map/ppermute | solution.py:362
  20.0 4.0 %collective-permute-start.3 = (bf16[1024,256]{1,0:T(8,128)(2,1)S(1)}, bf16[1024,256]{1,0:T(8,128)(2,1)}, u32[]{:S(2)}, u32[]{:S(2)}) collective-permute-start(bf16[1024,256]{1,0:T(8,128)(2,1)S(1)} %pad_maximum_fusion.refs_0_), channel_id=1, source_target_pairs={{0,14},{2,0},{4,2},{6,4},{8,6},{10,8},{12,10},{14,12},{1,15},{3,1}... | collective-permute-start | bytes 1572872 | tf_op jit(solution)/shard_map/ppermute | solution.py:363
  24.6 4.9 %sort_own.1 = bf16[8,128,512]{2,1,0:T(8,128)(2,1)} custom-call(s32[5]{0:T(128)} %stack.23.place_ref, s32[1,128]{1,0:T(1,128)} %order_ref.5, bf16[128,8192]{1,0:T(8,128)(2,1)} %x_ref.3), custom_call_target="tpu_custom_call" | custom-call | tf_op jit(solution)/shard_map/sort_own/pallas_call | solution.py:108
  29.4 6.6 %collective-permute-done.2.refs_7_ = bf16[1024,256]{1,0:T(8,128)(2,1)S(1)} collective-permute-done((bf16[1024,256]{1,0:T(8,128)(2,1)S(1)}, bf16[1024,256]{1,0:T(8,128)(2,1)S(1)}, u32[]{:S(2)}, u32[]{:S(2)}) %collective-permute-start.2) | collective-permute-done | bytes 524320 | tf_op jit(solution)/shard_map/ppermute | solution.py:362
  36.1 4.9 %all-to-all-start.1 = ((bf16[8,128,512]{2,1,0:T(8,128)(2,1)}), bf16[8,128,512]{2,1,0:T(8,128)(2,1)}, u32[]{:S(2)}, u32[]{:S(2)}) async-start(bf16[8,128,512]{2,1,0:T(8,128)(2,1)} %sort_own.1), calls=%async_computation.1 | async-start | bytes 2097152 | tf_op jit(solution)/shard_map/all_to_all | solution.py:365
  41.3 4.0 %collective-permute-start.6 = (bf16[1024,256]{1,0:T(8,128)(2,1)}, bf16[1024,256]{1,0:T(8,128)(2,1)}, u32[]{:S(2)}, u32[]{:S(2)}) collective-permute-start(bf16[1024,256]{1,0:T(8,128)(2,1)} %collective-permute-done.3.refs_1_), channel_id=1, source_target_pairs={{0,14},{2,0},{4,2},{6,4},{8,6},{10,8},{12,10},{14,12},{1,15},{3,1}... | collective-permute-start | bytes 1572872 | tf_op jit(solution)/shard_map/ppermute | solution.py:367
  45.3 4.7 %probs.1 = (f32[128,4096]{1,0:T(8,128)}, bf16[128,512]{1,0:T(8,128)(2,1)}, bf16[8,256,512]{2,1,0:T(8,128)(2,1)}) custom-call(s32[1,128]{1,0:T(1,128)} %seg_ref.1, bf16[128,4608]{1,0:T(8,128)(2,1)} %bitcast.7, bf16[128,4608]{1,0:T(8,128)(2,1)} %bitcast.8, bf16[128,4096]{1,0:T(8,128)(2,1)} %grad_ref.3), custom_call_target="tpu_custom_call" | custom-call | tf_op jit(solution)/shard_map/probs/pallas_call | solution.py:149
  50.0 4.9 %sort_other.1 = bf16[8,256,512]{2,1,0:T(8,128)(2,1)} custom-call(s32[5]{0:T(128)} %stack.23.place_ref, s32[1,128]{1,0:T(1,128)} %copy-done.15, bf16[128,8192]{1,0:T(8,128)(2,1)} %collective-permute-done.4.x_ref, bf16[8,256,512]{2,1,0:T(8,128)(2,1)} %get-tuple-element.51._), custom_call_target="tpu_custom_call", output_to_operand_aliasing={{}: (3, {})} | custom-call | tf_op jit(solution)/shard_map/sort_other/pallas_call | solution.py:108
  54.8 1.9 %collective-permute-done.5.refs_6_ = bf16[1024,256]{1,0:T(8,128)(2,1)S(1)} collective-permute-done((bf16[1024,256]{1,0:T(8,128)(2,1)S(1)}, bf16[1024,256]{1,0:T(8,128)(2,1)S(1)}, u32[]{:S(2)}, u32[]{:S(2)}) %collective-permute-start.5) | collective-permute-done | bytes 524320 | tf_op jit(solution)/shard_map/ppermute | solution.py:366
  57.5 4.5 %all-to-all-start.2 = ((bf16[8,256,512]{2,1,0:T(8,128)(2,1)}), bf16[8,256,512]{2,1,0:T(8,128)(2,1)S(1)}, u32[]{:S(2)}, u32[]{:S(2)}) async-start(bf16[8,256,512]{2,1,0:T(8,128)(2,1)} %sort_other.1), calls=%async_computation.2 | async-start | bytes 4194304 | tf_op jit(solution)/shard_map/all_to_all | solution.py:372
  62.1 2.7 %collective-permute-start.9 = (bf16[1024,256]{1,0:T(8,128)(2,1)}, bf16[1024,256]{1,0:T(8,128)(2,1)S(1)}, u32[]{:S(2)}, u32[]{:S(2)}) collective-permute-start(bf16[1024,256]{1,0:T(8,128)(2,1)} %collective-permute-done.6.refs_2_), channel_id=1, source_target_pairs={{0,14},{2,0},{4,2},{6,4},{8,6},{10,8},{12,10},{14,12},{1,15},{3,1}... | collective-permute-start | bytes 1572872 | tf_op jit(solution)/shard_map/ppermute | solution.py:374
  64.8 10.1 %collective-permute-done.7.refs_5_ = bf16[1024,256]{1,0:T(8,128)(2,1)S(1)} collective-permute-done((bf16[1024,256]{1,0:T(8,128)(2,1)}, bf16[1024,256]{1,0:T(8,128)(2,1)S(1)}, u32[]{:S(2)}, u32[]{:S(2)}) %collective-permute-start.7) | collective-permute-done | bytes 524320 | tf_op jit(solution)/shard_map/ppermute | solution.py:373
  76.5 10.2 %collective-permute-done.8.refs_4_ = bf16[1024,256]{1,0:T(8,128)(2,1)} collective-permute-done((bf16[1024,256]{1,0:T(8,128)(2,1)S(1)}, bf16[1024,256]{1,0:T(8,128)(2,1)}, u32[]{:S(2)}, u32[]{:S(2)}) %collective-permute-start.8) | collective-permute-done | bytes 524320 | tf_op jit(solution)/shard_map/ppermute | solution.py:375
  86.6 4.6 %all-to-all-done.2.both_ref = bf16[8,256,512]{2,1,0:T(8,128)(2,1)S(1)} async-done(((bf16[8,256,512]{2,1,0:T(8,128)(2,1)}), bf16[8,256,512]{2,1,0:T(8,128)(2,1)S(1)}, u32[]{:S(2)}, u32[]{:S(2)}) %all-to-all-start.2) | async-done | bytes 2097184 | tf_op jit(solution)/shard_map/all_to_all | solution.py:372
  91.3 2.3 %collective-permute-start.10 = (bf16[8,128,512]{2,1,0:T(8,128)(2,1)S(1)}, bf16[8,128,512]{2,1,0:T(8,128)(2,1)}, u32[]{:S(2)}, u32[]{:S(2)}) collective-permute-start(bf16[8,128,512]{2,1,0:T(8,128)(2,1)S(1)} %slice.3), channel_id=1, source_target_pairs={{0,16},{16,0},{1,17},{17,1},{2,18},{18,2},{3,19},{19,3},{4,20},{20... | collective-permute-start | bytes 3145736 | tf_op jit(solution)/shard_map/ppermute | solution.py:377
  93.5 2.4 %collective-permute-done.10.other_ref = bf16[8,128,512]{2,1,0:T(8,128)(2,1)} collective-permute-done((bf16[8,128,512]{2,1,0:T(8,128)(2,1)S(1)}, bf16[8,128,512]{2,1,0:T(8,128)(2,1)}, u32[]{:S(2)}, u32[]{:S(2)}) %collective-permute-start.10) | collective-permute-done | bytes 1048608 | tf_op jit(solution)/shard_map/ppermute | solution.py:377
  96.0 4.5 %weight_part.1 = bf16[16,32,512]{2,1,0:T(8,128)(2,1)} custom-call(s32[5]{0:T(128)} %stack.23.place_ref, bf16[8,128,512]{2,1,0:T(8,128)(2,1)} %all-to-all-done.1.own_ref, bf16[8,256,512]{2,1,0:T(8,128)(2,1)} %copy-done.2, bf16[8,128,512]{2,1,0:T(8,128)(2,1)} %collective-permute-done.10.other_ref), custom_call_target="tpu_custom_call" | custom-call | tf_op jit(solution)/shard_map/weight_part/pallas_call | solution.py:253
  101.4 7.3 %all-to-all-start.3 = ((bf16[16,32,512]{2,1,0:T(8,128)(2,1)}), bf16[16,32,512]{2,1,0:T(8,128)(2,1)S(1)}, u32[]{:S(2)}, u32[]{:S(2)}) async-start(bf16[16,32,512]{2,1,0:T(8,128)(2,1)} %weight_part.1), calls=%async_computation.3 | async-start | bytes 1048576 | tf_op jit(solution)/shard_map/all_to_all | solution.py:380
  110.9 1.6 %collective-permute-done.15.refs_12_ = bf16[1024,256]{1,0:T(8,128)(2,1)} collective-permute-done((bf16[1024,256]{1,0:T(8,128)(2,1)}, bf16[1024,256]{1,0:T(8,128)(2,1)}, u32[]{:S(2)}, u32[]{:S(2)}) %collective-permute-start.15) | collective-permute-done | bytes 524320 | tf_op jit(solution)/shard_map/ppermute | solution.py:383
  114.1 6.2 %values.1.v_ref = bf16[16,32,128]{2,1,0:T(8,128)(2,1)} custom-call(s32[5]{0:T(128)} %stack.23.place_ref, s32[1,128]{1,0:T(1,128)} %order_ref.5, bf16[128,8192]{1,0:T(8,128)(2,1)} %x_ref.3, bf16[1024,256]{1,0:T(8,128)(2,1)} %copy-done.4, bf16[1024,256]{1,0:T(8,128)(2,1)} %collective-permute-done.3.refs_1_, bf16[1024,256]{1,0:T(8,128)(2,1)} %collective-permute-done.6.refs_2_, ...), custom_call_target="tpu_custom_call" | custom-call | tf_op jit(solution)/shard_map/values/pallas_call | solution.py:313
  120.3 6.1 %all-to-all-done.3.shares_ref = bf16[16,32,512]{2,1,0:T(8,128)(2,1)S(1)} async-done(((bf16[16,32,512]{2,1,0:T(8,128)(2,1)}), bf16[16,32,512]{2,1,0:T(8,128)(2,1)S(1)}, u32[]{:S(2)}, u32[]{:S(2)}) %all-to-all-start.3) | async-done | bytes 524320 | tf_op jit(solution)/shard_map/all_to_all | solution.py:380
  127.2 2.0 %share.1 = bf16[16,32,640]{2,1,0:T(8,128)(2,1)} custom-call(bf16[16,32,512]{2,1,0:T(8,128)(2,1)} %copy-done.5, bf16[16,32,128]{2,1,0:T(8,128)(2,1)} %values.1.v_ref), custom_call_target="tpu_custom_call" | custom-call | tf_op jit(solution)/shard_map/share/pallas_call | solution.py:335
  129.1 5.9 %all-to-all-start.4 = ((bf16[16,32,640]{2,1,0:T(8,128)(2,1)}), bf16[16,32,640]{2,1,0:T(8,128)(2,1)S(1)}, u32[]{:S(2)}, u32[]{:S(2)}) async-start(bf16[16,32,640]{2,1,0:T(8,128)(2,1)} %share.1), calls=%async_computation.4 | async-start | bytes 1310720 | tf_op jit(solution)/shard_map/all_to_all | solution.py:391
  135.0 7.6 %input_grad.1 = bf16[128,8192]{1,0:T(8,128)(2,1)} custom-call(s32[5]{0:T(128)} %stack.23.place_ref, bf16[128,512]{1,0:T(8,128)(2,1)} %get-tuple-element.80.grad_ref, bf16[1024,256]{1,0:T(8,128)(2,1)} %copy-done.4, bf16[1024,256]{1,0:T(8,128)(2,1)} %collective-permute-done.3.refs_1_, bf16[1024,256]{1,0:T(8,128)(2,1)} %collective-permute-done.6.refs_2_, ...), custom_call_target="tpu_custom_call" | custom-call | tf_op jit(solution)/shard_map/input_grad/pallas_call | solution.py:313
  142.6 3.4 %all-to-all-done.4.v_ref.share_ref = bf16[16,32,640]{2,1,0:T(8,128)(2,1)S(1)} async-done(((bf16[16,32,640]{2,1,0:T(8,128)(2,1)}), bf16[16,32,640]{2,1,0:T(8,128)(2,1)S(1)}, u32[]{:S(2)}, u32[]{:S(2)}) %all-to-all-start.4) | async-done | bytes 655392 | tf_op jit(solution)/shard_map/all_to_all | solution.py:391
  146.8 5.2 %attend.1 = (bf16[128,4096]{1,0:T(8,128)(2,1)}, bf16[128,4096]{1,0:T(8,128)(2,1)}, bf16[128,512]{1,0:T(8,128)(2,1)}, f32[512,512]{1,0:T(8,128)}) custom-call(f32[128,4096]{1,0:T(8,128)} %get-tuple-element.49.probs_ref, bf16[128,4608]{1,0:T(8,128)(2,1)} %bitcast.9, bf16[128,4608]{1,0:T(8,128)(2,1)} %bitcast.10, bf16[16,32,640]{2,1,0:T(8,128)(2,1)} %copy-done.3, ...), custom_call_target="tpu_custom_call" | custom-call | tf_op jit(solution)/shard_map/attend/pallas_call | solution.py:204
  (61 shorter events, 10.0 us)
Async XLA Ops:
  1.7 8.8 %collective-permute-start = (bf16[512,256]{1,0:T(8,128)(2,1)S(1)}, bf16[512,256]{1,0:T(8,128)(2,1)S(1)}, u32[]{:S(2)}, u32[]{:S(2)}) collective-permute-start(bf16[512,256]{1,0:T(8,128)(2,1)S(1)} %constant_dynamic-slice_fusion), channel_id=1, source_target_pairs={{0,1},{1,0},{2,3},{3,2},{4,5},{5,4},{6,7},{7,6},{8,9},{9,8},{10,11... | collective-permute-start | bytes 786440 | tf_op jit(solution)/shard_map/ppermute | solution.py:351
  5.5 44.4 %collective-permute-start.4 = (bf16[128,8192]{1,0:T(8,128)(2,1)}, bf16[128,8192]{1,0:T(8,128)(2,1)}, u32[]{:S(2)}, u32[]{:S(2)}) collective-permute-start(bf16[128,8192]{1,0:T(8,128)(2,1)} %x_ref.3), channel_id=1, source_target_pairs={{0,16},{16,0},{1,17},{17,1},{2,18},{18,2},{3,19},{19,3},{4,20},{20... | collective-permute-start | bytes 6291464 | tf_op jit(solution)/shard_map/ppermute | solution.py:352
  6.5 3.7 %collective-permute-start.1 = (s32[1,128]{1,0:T(1,128)}, s32[1,128]{1,0:T(1,128)S(1)}, u32[]{:S(2)}, u32[]{:S(2)}) collective-permute-start(s32[1,128]{1,0:T(1,128)} %order_ref.5), channel_id=1, source_target_pairs={{0,16},{16,0},{1,17},{17,1},{2,18},{18,2},{3,19},{19,3},{4,20},{20... | collective-permute-start | bytes 1544 | tf_op jit(solution)/shard_map/ppermute | solution.py:353
  10.2 19.2 %copy-start.15 = (s32[1,128]{1,0:T(1,128)}, s32[1,128]{1,0:T(1,128)S(1)}, u32[]{:S(2)}) copy-start(s32[1,128]{1,0:T(1,128)S(1)} %collective-permute-done.1.order_ref) | copy-start | bytes 1540
  10.5 25.6 %all-to-all-start = ((bf16[16,8,4608]{2,1,0:T(8,128)(2,1)}), bf16[16,8,4608]{2,1,0:T(8,128)(2,1)S(1)}, u32[]{:S(2)}, u32[]{:S(2)}) async-start(bf16[16,8,4608]{2,1,0:T(8,128)(2,1)} %bitcast.11), calls=%async_computation | async-start | bytes 2359296 | tf_op jit(solution)/shard_map/all_to_all | solution.py:357
  18.2 82.3 %copy-start.4 = (bf16[1024,256]{1,0:T(8,128)(2,1)}, bf16[1024,256]{1,0:T(8,128)(2,1)S(1)}, u32[]{:S(2)}) copy-start(bf16[1024,256]{1,0:T(8,128)(2,1)S(1)} %pad_maximum_fusion.refs_0_) | copy-start | bytes 1572868
  18.2 17.8 %collective-permute-start.2 = (bf16[1024,256]{1,0:T(8,128)(2,1)S(1)}, bf16[1024,256]{1,0:T(8,128)(2,1)S(1)}, u32[]{:S(2)}, u32[]{:S(2)}) collective-permute-start(bf16[1024,256]{1,0:T(8,128)(2,1)S(1)} %pad_maximum_fusion.refs_0_), channel_id=1, source_target_pairs={{0,2},{2,4},{4,6},{6,8},{8,10},{10,12},{12,14},{14,0},{1,3},{3,5},... | collective-permute-start | bytes 1572872 | tf_op jit(solution)/shard_map/ppermute | solution.py:362
  20.0 16.1 %collective-permute-start.3 = (bf16[1024,256]{1,0:T(8,128)(2,1)S(1)}, bf16[1024,256]{1,0:T(8,128)(2,1)}, u32[]{:S(2)}, u32[]{:S(2)}) collective-permute-start(bf16[1024,256]{1,0:T(8,128)(2,1)S(1)} %pad_maximum_fusion.refs_0_), channel_id=1, source_target_pairs={{0,14},{2,0},{4,2},{6,4},{8,6},{10,8},{12,10},{14,12},{1,15},{3,1}... | collective-permute-start | bytes 1572872 | tf_op jit(solution)/shard_map/ppermute | solution.py:363
  36.1 13.9 %copy-start.6 = (bf16[1024,256]{1,0:T(8,128)(2,1)}, bf16[1024,256]{1,0:T(8,128)(2,1)S(1)}, u32[]{:S(2)}) copy-start(bf16[1024,256]{1,0:T(8,128)(2,1)S(1)} %collective-permute-done.2.refs_7_) | copy-start | bytes 1572868
  36.1 9.2 %copy-start.1 = (bf16[16,8,4608]{2,1,0:T(8,128)(2,1)}, bf16[16,8,4608]{2,1,0:T(8,128)(2,1)S(1)}, u32[]{:S(2)}) copy-start(bf16[16,8,4608]{2,1,0:T(8,128)(2,1)S(1)} %all-to-all-done) | copy-start | bytes 3538948
  36.1 21.4 %all-to-all-start.1 = ((bf16[8,128,512]{2,1,0:T(8,128)(2,1)}), bf16[8,128,512]{2,1,0:T(8,128)(2,1)}, u32[]{:S(2)}, u32[]{:S(2)}) async-start(bf16[8,128,512]{2,1,0:T(8,128)(2,1)} %sort_own.1), calls=%async_computation.1 | async-start | bytes 2097152 | tf_op jit(solution)/shard_map/all_to_all | solution.py:365
  41.0 15.7 %collective-permute-start.5 = (bf16[1024,256]{1,0:T(8,128)(2,1)S(1)}, bf16[1024,256]{1,0:T(8,128)(2,1)S(1)}, u32[]{:S(2)}, u32[]{:S(2)}) collective-permute-start(bf16[1024,256]{1,0:T(8,128)(2,1)S(1)} %collective-permute-done.2.refs_7_), channel_id=1, source_target_pairs={{0,2},{2,4},{4,6},{6,8},{8,10},{10,12},{12,14},{14,0},{1,3},{3,5},... | collective-permute-start | bytes 1572872 | tf_op jit(solution)/shard_map/ppermute | solution.py:366
  41.3 16.3 %collective-permute-start.6 = (bf16[1024,256]{1,0:T(8,128)(2,1)}, bf16[1024,256]{1,0:T(8,128)(2,1)}, u32[]{:S(2)}, u32[]{:S(2)}) collective-permute-start(bf16[1024,256]{1,0:T(8,128)(2,1)} %collective-permute-done.3.refs_1_), channel_id=1, source_target_pairs={{0,14},{2,0},{4,2},{6,4},{8,6},{10,8},{12,10},{14,12},{1,15},{3,1}... | collective-permute-start | bytes 1572872 | tf_op jit(solution)/shard_map/ppermute | solution.py:367
  57.5 33.7 %all-to-all-start.2 = ((bf16[8,256,512]{2,1,0:T(8,128)(2,1)}), bf16[8,256,512]{2,1,0:T(8,128)(2,1)S(1)}, u32[]{:S(2)}, u32[]{:S(2)}) async-start(bf16[8,256,512]{2,1,0:T(8,128)(2,1)} %sort_other.1), calls=%async_computation.2 | async-start | bytes 4194304 | tf_op jit(solution)/shard_map/all_to_all | solution.py:372
  62.1 12.8 %collective-permute-start.7 = (bf16[1024,256]{1,0:T(8,128)(2,1)}, bf16[1024,256]{1,0:T(8,128)(2,1)S(1)}, u32[]{:S(2)}, u32[]{:S(2)}) collective-permute-start(bf16[1024,256]{1,0:T(8,128)(2,1)} %copy-done.7), channel_id=1, source_target_pairs={{0,2},{2,4},{4,6},{6,8},{8,10},{10,12},{12,14},{14,0},{1,3},{3,5},... | collective-permute-start | bytes 1572872 | tf_op jit(solution)/shard_map/ppermute | solution.py:373
  62.1 12.8 %collective-permute-start.9 = (bf16[1024,256]{1,0:T(8,128)(2,1)}, bf16[1024,256]{1,0:T(8,128)(2,1)S(1)}, u32[]{:S(2)}, u32[]{:S(2)}) collective-permute-start(bf16[1024,256]{1,0:T(8,128)(2,1)} %collective-permute-done.6.refs_2_), channel_id=1, source_target_pairs={{0,14},{2,0},{4,2},{6,4},{8,6},{10,8},{12,10},{14,12},{1,15},{3,1}... | collective-permute-start | bytes 1572872 | tf_op jit(solution)/shard_map/ppermute | solution.py:374
  74.9 11.8 %collective-permute-start.8 = (bf16[1024,256]{1,0:T(8,128)(2,1)S(1)}, bf16[1024,256]{1,0:T(8,128)(2,1)}, u32[]{:S(2)}, u32[]{:S(2)}) collective-permute-start(bf16[1024,256]{1,0:T(8,128)(2,1)S(1)} %collective-permute-done.7.refs_5_), channel_id=1, source_target_pairs={{0,2},{2,4},{4,6},{6,8},{8,10},{10,12},{12,14},{14,0},{1,3},{3,5},... | collective-permute-start | bytes 1572872 | tf_op jit(solution)/shard_map/ppermute | solution.py:375
  91.2 4.8 %copy-start.2 = (bf16[8,256,512]{2,1,0:T(8,128)(2,1)}, bf16[8,256,512]{2,1,0:T(8,128)(2,1)S(1)}, u32[]{:S(2)}) copy-start(bf16[8,256,512]{2,1,0:T(8,128)(2,1)S(1)} %all-to-all-done.2.both_ref) | copy-start | bytes 6291460
  91.3 4.7 %collective-permute-start.10 = (bf16[8,128,512]{2,1,0:T(8,128)(2,1)S(1)}, bf16[8,128,512]{2,1,0:T(8,128)(2,1)}, u32[]{:S(2)}, u32[]{:S(2)}) collective-permute-start(bf16[8,128,512]{2,1,0:T(8,128)(2,1)S(1)} %slice.3), channel_id=1, source_target_pairs={{0,16},{16,0},{1,17},{17,1},{2,18},{18,2},{3,19},{19,3},{4,20},{20... | collective-permute-start | bytes 3145736 | tf_op jit(solution)/shard_map/ppermute | solution.py:377
  100.5 8.8 %collective-permute-start.11 = (bf16[1024,256]{1,0:T(8,128)(2,1)S(1)}, bf16[1024,256]{1,0:T(8,128)(2,1)S(1)}, u32[]{:S(2)}, u32[]{:S(2)}) collective-permute-start(bf16[1024,256]{1,0:T(8,128)(2,1)S(1)} %pad_maximum_fusion.refs_0_), channel_id=1, source_target_pairs={{0,16},{16,0},{1,17},{17,1},{2,18},{18,2},{3,19},{19,3},{4,20},{20... | collective-permute-start | bytes 1572872 | tf_op jit(solution)/shard_map/ppermute | solution.py:383
  100.9 8.8 %collective-permute-start.12 = (bf16[1024,256]{1,0:T(8,128)(2,1)}, bf16[1024,256]{1,0:T(8,128)(2,1)S(1)}, u32[]{:S(2)}, u32[]{:S(2)}) collective-permute-start(bf16[1024,256]{1,0:T(8,128)(2,1)} %collective-permute-done.3.refs_1_), channel_id=1, source_target_pairs={{0,16},{16,0},{1,17},{17,1},{2,18},{18,2},{3,19},{19,3},{4,20},{20... | collective-permute-start | bytes 1572872 | tf_op jit(solution)/shard_map/ppermute | solution.py:383
  101.0 8.8 %collective-permute-start.13 = (bf16[1024,256]{1,0:T(8,128)(2,1)}, bf16[1024,256]{1,0:T(8,128)(2,1)S(1)}, u32[]{:S(2)}, u32[]{:S(2)}) collective-permute-start(bf16[1024,256]{1,0:T(8,128)(2,1)} %collective-permute-done.6.refs_2_), channel_id=1, source_target_pairs={{0,16},{16,0},{1,17},{17,1},{2,18},{18,2},{3,19},{19,3},{4,20},{20... | collective-permute-start | bytes 1572872 | tf_op jit(solution)/shard_map/ppermute | solution.py:383
  101.4 25.0 %all-to-all-start.3 = ((bf16[16,32,512]{2,1,0:T(8,128)(2,1)}), bf16[16,32,512]{2,1,0:T(8,128)(2,1)S(1)}, u32[]{:S(2)}, u32[]{:S(2)}) async-start(bf16[16,32,512]{2,1,0:T(8,128)(2,1)} %weight_part.1), calls=%async_computation.3 | async-start | bytes 1048576 | tf_op jit(solution)/shard_map/all_to_all | solution.py:380
  108.7 2.3 %collective-permute-start.14 = (bf16[1024,256]{1,0:T(8,128)(2,1)}, bf16[1024,256]{1,0:T(8,128)(2,1)S(1)}, u32[]{:S(2)}, u32[]{:S(2)}) collective-permute-start(bf16[1024,256]{1,0:T(8,128)(2,1)} %copy-done.9), channel_id=1, source_target_pairs={{0,16},{16,0},{1,17},{17,1},{2,18},{18,2},{3,19},{19,3},{4,20},{20... | collective-permute-start | bytes 1572872 | tf_op jit(solution)/shard_map/ppermute | solution.py:383
  109.2 3.4 %collective-permute-start.15 = (bf16[1024,256]{1,0:T(8,128)(2,1)}, bf16[1024,256]{1,0:T(8,128)(2,1)}, u32[]{:S(2)}, u32[]{:S(2)}) collective-permute-start(bf16[1024,256]{1,0:T(8,128)(2,1)} %collective-permute-done.8.refs_4_), channel_id=1, source_target_pairs={{0,16},{16,0},{1,17},{17,1},{2,18},{18,2},{3,19},{19,3},{4,20},{20... | collective-permute-start | bytes 1572872 | tf_op jit(solution)/shard_map/ppermute | solution.py:383
  109.3 4.8 %copy-start.10 = (bf16[1024,256]{1,0:T(8,128)(2,1)}, bf16[1024,256]{1,0:T(8,128)(2,1)S(1)}, u32[]{:S(2)}) copy-start(bf16[1024,256]{1,0:T(8,128)(2,1)S(1)} %collective-permute-done.11.refs_8_) | copy-start | bytes 1572868
  109.3 3.3 %collective-permute-start.16 = (bf16[1024,256]{1,0:T(8,128)(2,1)}, bf16[1024,256]{1,0:T(8,128)(2,1)S(1)}, u32[]{:S(2)}, u32[]{:S(2)}) collective-permute-start(bf16[1024,256]{1,0:T(8,128)(2,1)} %copy-done.8), channel_id=1, source_target_pairs={{0,16},{16,0},{1,17},{17,1},{2,18},{18,2},{3,19},{19,3},{4,20},{20... | collective-permute-start | bytes 1572872 | tf_op jit(solution)/shard_map/ppermute | solution.py:383
  109.7 4.4 %copy-start.11 = (bf16[1024,256]{1,0:T(8,128)(2,1)}, bf16[1024,256]{1,0:T(8,128)(2,1)S(1)}, u32[]{:S(2)}) copy-start(bf16[1024,256]{1,0:T(8,128)(2,1)S(1)} %collective-permute-done.12.refs_9_) | copy-start | bytes 1572868
  109.7 3.6 %collective-permute-start.17 = (bf16[1024,256]{1,0:T(8,128)(2,1)}, bf16[1024,256]{1,0:T(8,128)(2,1)}, u32[]{:S(2)}, u32[]{:S(2)}) collective-permute-start(bf16[1024,256]{1,0:T(8,128)(2,1)} %copy-done.7), channel_id=1, source_target_pairs={{0,16},{16,0},{1,17},{17,1},{2,18},{18,2},{3,19},{19,3},{4,20},{20... | collective-permute-start | bytes 1572872 | tf_op jit(solution)/shard_map/ppermute | solution.py:383
  109.8 4.3 %copy-start.12 = (bf16[1024,256]{1,0:T(8,128)(2,1)}, bf16[1024,256]{1,0:T(8,128)(2,1)S(1)}, u32[]{:S(2)}) copy-start(bf16[1024,256]{1,0:T(8,128)(2,1)S(1)} %collective-permute-done.13.refs_10_) | copy-start | bytes 1572868
  109.8 4.2 %collective-permute-start.18 = (bf16[1024,256]{1,0:T(8,128)(2,1)}, bf16[1024,256]{1,0:T(8,128)(2,1)}, u32[]{:S(2)}, u32[]{:S(2)}) collective-permute-start(bf16[1024,256]{1,0:T(8,128)(2,1)} %copy-done.6), channel_id=1, source_target_pairs={{0,16},{16,0},{1,17},{17,1},{2,18},{18,2},{3,19},{19,3},{4,20},{20... | collective-permute-start | bytes 1572872 | tf_op jit(solution)/shard_map/ppermute | solution.py:383
  129.1 16.8 %all-to-all-start.4 = ((bf16[16,32,640]{2,1,0:T(8,128)(2,1)}), bf16[16,32,640]{2,1,0:T(8,128)(2,1)S(1)}, u32[]{:S(2)}, u32[]{:S(2)}) async-start(bf16[16,32,640]{2,1,0:T(8,128)(2,1)} %share.1), calls=%async_computation.4 | async-start | bytes 1310720 | tf_op jit(solution)/shard_map/all_to_all | solution.py:391
  (8 other events, 9.7 us)

commit v3 on v2

--- a/solution.py
+++ b/solution.py
@@ -18,6 +18,7 @@
 SUB = D // N_DP // N_SHARD
 FACTOR = HD ** (-0.5)
 VMEM = 60 * 1024 * 1024
+VMEM_LATE = 65024 * 1024
 LIGHT = pl.CostEstimate(flops=0, bytes_accessed=0, transcendentals=0)
 
 FINE = (("x", 4), ("yl", 2), ("c", 2), ("z", 8), ("yh", 2))
@@ -221,31 +222,25 @@
             jax.ShapeDtypeStruct((KVW, KVW), jnp.float32),
         ],
         cost_estimate=LIGHT,
-        compiler_params=pltpu.CompilerParams(vmem_limit_bytes=VMEM),
+        compiler_params=pltpu.CompilerParams(vmem_limit_bytes=VMEM_LATE),
         name="attend",
     )(probs, moved, moved, got, got, out_grad)
 
 
-def weight_kernel(place_ref, own_ref, both_ref, other_ref, out_ref, wide_ref, total_ref):
+def weight_kernel(place_ref, own_ref, both_ref, other_ref, out_ref, wide_ref):
     core = place_ref[2]
     for k in range(PEERS):
         wide_ref[k * 2 + core] = own_ref[k].astype(jnp.float32)
         wide_ref[k * 2 + 1 - core] = both_ref[k, ROWS:, :].astype(jnp.float32)
-    for step in range(PEERS // 2):
-        lhs, rhs = [], []
-        for at in (step * 2, step * 2 + 1):
-            for co in range(2):
-                to = at * 2 + (core ^ co)
-                rows = pl.ds(pl.multiple_of(to * 8, 8), 8)
-                lhs += [wide_ref[source, rows, :] for source in range(N_DP)]
-                rhs.append(other_ref[at] if co else both_ref[at, :ROWS, :])
-        part = dot(jnp.concatenate(lhs, axis=0).astype(jnp.bfloat16), jnp.concatenate(rhs, axis=0), TN)
-        if step == 0:
-            total_ref[...] = part
-        elif step < PEERS // 2 - 1:
-            total_ref[...] += part
-        else:
-            out_ref[...] = (total_ref[...] + part).astype(jnp.bfloat16).reshape(out_ref.shape)
+    lhs, rhs = [], []
+    for at in range(PEERS):
+        for co in range(2):
+            to = at * 2 + (core ^ co)
+            rows = pl.ds(pl.multiple_of(to * 8, 8), 8)
+            lhs += [wide_ref[source, rows, :] for source in range(N_DP)]
+            rhs.append(other_ref[at] if co else both_ref[at, :ROWS, :])
+    total = dot(jnp.concatenate(lhs, axis=0).astype(jnp.bfloat16), jnp.concatenate(rhs, axis=0), TN)
+    out_ref[...] = total.astype(jnp.bfloat16).reshape(out_ref.shape)
 
 
 def weight_part(place, own, both, other):
@@ -257,7 +252,6 @@
         out_shape=jax.ShapeDtypeStruct((N_SHARD, SUB, KVW), jnp.bfloat16),
         scratch_shapes=[
             pltpu.VMEM((N_DP, ROWS, KVW), jnp.float32),
-            pltpu.VMEM((KVW, KVW), jnp.float32),
         ],
         cost_estimate=LIGHT,
         compiler_params=pltpu.CompilerParams(vmem_limit_bytes=VMEM),
@@ -316,7 +310,7 @@
         out_specs=vmem,
         out_shape=jax.ShapeDtypeStruct(out_shape, jnp.bfloat16),
         cost_estimate=LIGHT,
-        compiler_params=pltpu.CompilerParams(vmem_limit_bytes=VMEM),
+        compiler_params=pltpu.CompilerParams(vmem_limit_bytes=VMEM_LATE),
         name=name,
     )(place, *operands)
 
@@ -332,11 +326,15 @@
 
 
 def make_share(shares, sent_v):
+    whole = lambda i: (0, 0, 0)
     return pl.pallas_call(
         share_kernel,
+        grid=(1,),
+        in_specs=[pl.BlockSpec(shares.shape, whole), pl.BlockSpec(sent_v.shape, whole)],
+        out_specs=pl.BlockSpec((N_DP, SUB, KVW + HD), whole),
         out_shape=jax.ShapeDtypeStruct((N_DP, SUB, KVW + HD), jnp.bfloat16),
         cost_estimate=LIGHT,
-        compiler_params=pltpu.CompilerParams(vmem_limit_bytes=VMEM),
+        compiler_params=pltpu.CompilerParams(vmem_limit_bytes=VMEM_LATE),
         name="share",
     )(shares, sent_v)
 

time: 153 us -> 152 us (level)
    unnamed x32 -> x30, local copies, waits for them, and re-layouts: 5.1 us -> 3.31 us
where the time goes in v3:
time: 152 us; the launch traced here: 151 us
  starting transfers between devices  53.2 us (35%)
  waiting for transfers between devices  49.5 us (33%)
  Pallas kernels  42.7 us (28%)
  local copies, waits for them, and re-layouts  5.01 us (3%)
    pallas_call x2, Pallas kernels, with_weight(): pl.pallas_call(kernel, in_specs=[pl.BlockSpec(memory_space=pltpu.SMEM)] +...  13.8 us
    ppermute x1, waiting for transfers between devices, per_device(): up.append(lax.ppermute(up[3], 'z', right))  10.2 us
    ppermute x1, waiting for transfers between devices, per_device(): up.append(lax.ppermute(up[2], 'z', right))  10.1 us
    pallas_call x2, Pallas kernels, sort_x(): pl.pallas_call(sort_own_kernel if own else sort_other_kernel, grid=(4,),...  9.74 us
    all_to_all x1, starting transfers between devices, per_device(): lax.all_to_all(sent.reshape(N_DP, ROWS // N_DP, HQW + KVW), DP, split_axi...  7.66 us
    all_to_all x1, starting transfers between devices, per_device(): lax.all_to_all(partial, SHARD, split_axis=0, concat_axis=0, tiled=True)  7.32 us
    ppermute x1, waiting for transfers between devices, per_device(): up.append(lax.ppermute(up[0], 'z', right))  6.54 us
    all_to_all x1, starting transfers between devices, per_device(): lax.all_to_all(make_share(shares, sent_v), DP, split_axis=0, concat_axis=...  6.49 us
  transfers between devices with their start and end apart: 24, of which 14 were waited for; matrix products, arithmetic and copies ran while one was open for 0% of the time, Pallas kernels for 20%

profile of v3, /device:TPU:1, one launch (start us, length us, event | category | flops | bytes accessed | tf_op | source)
XLA Modules:
  0.0 151.3 jit_solution(18386570499484316026)
XLA Ops:
  0.6 1.0 constant_dynamic-slice_fusion
  1.6 3.8 %collective-permute-start = (bf16[512,256]{1,0:T(8,128)(2,1)S(1)}, bf16[512,256]{1,0:T(8,128)(2,1)S(1)}, u32[]{:S(2)}, u32[]{:S(2)}) collective-permute-start(bf16[512,256]{1,0:T(8,128)(2,1)S(1)} %constant_dynamic-slice_fusion), channel_id=1, source_target_pairs={{0,1},{1,0},{2,3},{3,2},{4,5},{5,4},{6,7},{7,6},{8,9},{9,8},{10,11... | collective-permute-start | bytes 786440 | tf_op jit(solution)/shard_map/ppermute | solution.py:349
  5.4 1.0 collective-permute-start.4
  6.4 2.7 %sort_qk.1 = bf16[128,4608]{1,0:T(8,128)(2,1)} custom-call(s32[1,128]{1,0:T(1,128)} %order_ref.5, bf16[128,4096]{1,0:T(8,128)(2,1)} %q_ref.1, bf16[128,512]{1,0:T(8,128)(2,1)} %k_ref.1), custom_call_target="tpu_custom_call" | custom-call | tf_op jit(solution)/shard_map/sort_qk/pallas_call | solution.py:53
  9.2 1.0 collective-permute-done.1.order_ref
  10.4 7.7 %all-to-all-start = ((bf16[16,8,4608]{2,1,0:T(8,128)(2,1)}), bf16[16,8,4608]{2,1,0:T(8,128)(2,1)S(1)}, u32[]{:S(2)}, u32[]{:S(2)}) async-start(bf16[16,8,4608]{2,1,0:T(8,128)(2,1)} %bitcast.11), calls=%async_computation | async-start | bytes 2359296 | tf_op jit(solution)/shard_map/all_to_all | solution.py:355
  18.1 1.7 %collective-permute-start.2 = (bf16[1024,256]{1,0:T(8,128)(2,1)S(1)}, bf16[1024,256]{1,0:T(8,128)(2,1)S(1)}, u32[]{:S(2)}, u32[]{:S(2)}) collective-permute-start(bf16[1024,256]{1,0:T(8,128)(2,1)S(1)} %pad_maximum_fusion.refs_0_), channel_id=1, source_target_pairs={{0,2},{2,4},{4,6},{6,8},{8,10},{10,12},{12,14},{14,0},{1,3},{3,5},... | collective-permute-start | bytes 1572872 | tf_op jit(solution)/shard_map/ppermute | solution.py:360
  19.9 4.0 %collective-permute-start.3 = (bf16[1024,256]{1,0:T(8,128)(2,1)S(1)}, bf16[1024,256]{1,0:T(8,128)(2,1)}, u32[]{:S(2)}, u32[]{:S(2)}) collective-permute-start(bf16[1024,256]{1,0:T(8,128)(2,1)S(1)} %pad_maximum_fusion.refs_0_), channel_id=1, source_target_pairs={{0,14},{2,0},{4,2},{6,4},{8,6},{10,8},{12,10},{14,12},{1,15},{3,1}... | collective-permute-start | bytes 1572872 | tf_op jit(solution)/shard_map/ppermute | solution.py:361
  24.6 4.9 %sort_own.1 = bf16[8,128,512]{2,1,0:T(8,128)(2,1)} custom-call(s32[5]{0:T(128)} %stack.23.place_ref, s32[1,128]{1,0:T(1,128)} %order_ref.5, bf16[128,8192]{1,0:T(8,128)(2,1)} %x_ref.3), custom_call_target="tpu_custom_call" | custom-call | tf_op jit(solution)/shard_map/sort_own/pallas_call | solution.py:109
  29.4 6.5 %collective-permute-done.2.refs_7_ = bf16[1024,256]{1,0:T(8,128)(2,1)S(1)} collective-permute-done((bf16[1024,256]{1,0:T(8,128)(2,1)S(1)}, bf16[1024,256]{1,0:T(8,128)(2,1)S(1)}, u32[]{:S(2)}, u32[]{:S(2)}) %collective-permute-start.2) | collective-permute-done | bytes 524320 | tf_op jit(solution)/shard_map/ppermute | solution.py:360
  36.0 4.9 %all-to-all-start.1 = ((bf16[8,128,512]{2,1,0:T(8,128)(2,1)}), bf16[8,128,512]{2,1,0:T(8,128)(2,1)}, u32[]{:S(2)}, u32[]{:S(2)}) async-start(bf16[8,128,512]{2,1,0:T(8,128)(2,1)} %sort_own.1), calls=%async_computation.1 | async-start | bytes 2097152 | tf_op jit(solution)/shard_map/all_to_all | solution.py:363
  41.1 4.0 %collective-permute-start.6 = (bf16[1024,256]{1,0:T(8,128)(2,1)}, bf16[1024,256]{1,0:T(8,128)(2,1)}, u32[]{:S(2)}, u32[]{:S(2)}) collective-permute-start(bf16[1024,256]{1,0:T(8,128)(2,1)} %collective-permute-done.3.refs_1_), channel_id=1, source_target_pairs={{0,14},{2,0},{4,2},{6,4},{8,6},{10,8},{12,10},{14,12},{1,15},{3,1}... | collective-permute-start | bytes 1572872 | tf_op jit(solution)/shard_map/ppermute | solution.py:365
  45.2 4.7 %probs.1 = (f32[128,4096]{1,0:T(8,128)}, bf16[128,512]{1,0:T(8,128)(2,1)}, bf16[8,256,512]{2,1,0:T(8,128)(2,1)}) custom-call(s32[1,128]{1,0:T(1,128)} %seg_ref.1, bf16[128,4608]{1,0:T(8,128)(2,1)} %bitcast.7, bf16[128,4608]{1,0:T(8,128)(2,1)} %bitcast.8, bf16[128,4096]{1,0:T(8,128)(2,1)} %grad_ref.3), custom_call_target="tpu_custom_call" | custom-call | tf_op jit(solution)/shard_map/probs/pallas_call | solution.py:150
  49.8 4.9 %sort_other.1 = bf16[8,256,512]{2,1,0:T(8,128)(2,1)} custom-call(s32[5]{0:T(128)} %stack.23.place_ref, s32[1,128]{1,0:T(1,128)} %copy-done.14, bf16[128,8192]{1,0:T(8,128)(2,1)} %collective-permute-done.4.x_ref, bf16[8,256,512]{2,1,0:T(8,128)(2,1)} %get-tuple-element.51._), custom_call_target="tpu_custom_call", output_to_operand_aliasing={{}: (3, {})} | custom-call | tf_op jit(solution)/shard_map/sort_other/pallas_call | solution.py:109
  54.7 1.9 %collective-permute-done.5.refs_6_ = bf16[1024,256]{1,0:T(8,128)(2,1)S(1)} collective-permute-done((bf16[1024,256]{1,0:T(8,128)(2,1)S(1)}, bf16[1024,256]{1,0:T(8,128)(2,1)S(1)}, u32[]{:S(2)}, u32[]{:S(2)}) %collective-permute-start.5) | collective-permute-done | bytes 524320 | tf_op jit(solution)/shard_map/ppermute | solution.py:364
  57.4 4.5 %all-to-all-start.2 = ((bf16[8,256,512]{2,1,0:T(8,128)(2,1)}), bf16[8,256,512]{2,1,0:T(8,128)(2,1)S(1)}, u32[]{:S(2)}, u32[]{:S(2)}) async-start(bf16[8,256,512]{2,1,0:T(8,128)(2,1)} %sort_other.1), calls=%async_computation.2 | async-start | bytes 4194304 | tf_op jit(solution)/shard_map/all_to_all | solution.py:370
  62.0 2.7 %collective-permute-start.9 = (bf16[1024,256]{1,0:T(8,128)(2,1)}, bf16[1024,256]{1,0:T(8,128)(2,1)S(1)}, u32[]{:S(2)}, u32[]{:S(2)}) collective-permute-start(bf16[1024,256]{1,0:T(8,128)(2,1)} %collective-permute-done.6.refs_2_), channel_id=1, source_target_pairs={{0,14},{2,0},{4,2},{6,4},{8,6},{10,8},{12,10},{14,12},{1,15},{3,1}... | collective-permute-start | bytes 1572872 | tf_op jit(solution)/shard_map/ppermute | solution.py:372
  64.6 10.1 %collective-permute-done.7.refs_5_ = bf16[1024,256]{1,0:T(8,128)(2,1)S(1)} collective-permute-done((bf16[1024,256]{1,0:T(8,128)(2,1)}, bf16[1024,256]{1,0:T(8,128)(2,1)S(1)}, u32[]{:S(2)}, u32[]{:S(2)}) %collective-permute-start.7) | collective-permute-done | bytes 524320 | tf_op jit(solution)/shard_map/ppermute | solution.py:371
  76.3 10.2 %collective-permute-done.8.refs_4_ = bf16[1024,256]{1,0:T(8,128)(2,1)} collective-permute-done((bf16[1024,256]{1,0:T(8,128)(2,1)S(1)}, bf16[1024,256]{1,0:T(8,128)(2,1)}, u32[]{:S(2)}, u32[]{:S(2)}) %collective-permute-start.8) | collective-permute-done | bytes 524320 | tf_op jit(solution)/shard_map/ppermute | solution.py:373
  86.5 4.6 %all-to-all-done.2.both_ref = bf16[8,256,512]{2,1,0:T(8,128)(2,1)S(1)} async-done(((bf16[8,256,512]{2,1,0:T(8,128)(2,1)}), bf16[8,256,512]{2,1,0:T(8,128)(2,1)S(1)}, u32[]{:S(2)}, u32[]{:S(2)}) %all-to-all-start.2) | async-done | bytes 2097184 | tf_op jit(solution)/shard_map/all_to_all | solution.py:370
  91.2 2.3 %collective-permute-start.10 = (bf16[8,128,512]{2,1,0:T(8,128)(2,1)S(1)}, bf16[8,128,512]{2,1,0:T(8,128)(2,1)}, u32[]{:S(2)}, u32[]{:S(2)}) collective-permute-start(bf16[8,128,512]{2,1,0:T(8,128)(2,1)S(1)} %slice.3), channel_id=1, source_target_pairs={{0,16},{16,0},{1,17},{17,1},{2,18},{18,2},{3,19},{19,3},{4,20},{20... | collective-permute-start | bytes 3145736 | tf_op jit(solution)/shard_map/ppermute | solution.py:375
  93.4 2.4 %collective-permute-done.10.other_ref = bf16[8,128,512]{2,1,0:T(8,128)(2,1)} collective-permute-done((bf16[8,128,512]{2,1,0:T(8,128)(2,1)S(1)}, bf16[8,128,512]{2,1,0:T(8,128)(2,1)}, u32[]{:S(2)}, u32[]{:S(2)}) %collective-permute-start.10) | collective-permute-done | bytes 1048608 | tf_op jit(solution)/shard_map/ppermute | solution.py:375
  95.8 4.5 %weight_part.1 = bf16[16,32,512]{2,1,0:T(8,128)(2,1)} custom-call(s32[5]{0:T(128)} %stack.23.place_ref, bf16[8,128,512]{2,1,0:T(8,128)(2,1)} %all-to-all-done.1.own_ref, bf16[8,256,512]{2,1,0:T(8,128)(2,1)} %copy-done.1, bf16[8,128,512]{2,1,0:T(8,128)(2,1)} %collective-permute-done.10.other_ref), custom_call_target="tpu_custom_call" | custom-call | tf_op jit(solution)/shard_map/weight_part/pallas_call | solution.py:248
  101.3 7.3 %all-to-all-start.3 = ((bf16[16,32,512]{2,1,0:T(8,128)(2,1)}), bf16[16,32,512]{2,1,0:T(8,128)(2,1)}, u32[]{:S(2)}, u32[]{:S(2)}) async-start(bf16[16,32,512]{2,1,0:T(8,128)(2,1)} %weight_part.1), calls=%async_computation.3 | async-start | bytes 1048576 | tf_op jit(solution)/shard_map/all_to_all | solution.py:378
  111.6 1.5 collective-permute-done.16.refs_13_
  114.8 6.2 %values.1.v_ref = bf16[16,32,128]{2,1,0:T(8,128)(2,1)} custom-call(s32[5]{0:T(128)} %stack.23.place_ref, s32[1,128]{1,0:T(1,128)} %order_ref.5, bf16[128,8192]{1,0:T(8,128)(2,1)} %x_ref.3, bf16[1024,256]{1,0:T(8,128)(2,1)} %copy-done.2, bf16[1024,256]{1,0:T(8,128)(2,1)} %collective-permute-done.3.refs_1_, bf16[1024,256]{1,0:T(8,128)(2,1)} %collective-permute-done.6.refs_2_, ...), custom_call_target="tpu_custom_call" | custom-call | tf_op jit(solution)/shard_map/values/pallas_call | solution.py:307
  121.0 5.4 %all-to-all-done.3.shares_ref = bf16[16,32,512]{2,1,0:T(8,128)(2,1)} async-done(((bf16[16,32,512]{2,1,0:T(8,128)(2,1)}), bf16[16,32,512]{2,1,0:T(8,128)(2,1)}, u32[]{:S(2)}, u32[]{:S(2)}) %all-to-all-start.3) | async-done | bytes 524320 | tf_op jit(solution)/shard_map/all_to_all | solution.py:378
  126.4 2.0 %share.1 = bf16[16,32,640]{2,1,0:T(8,128)(2,1)} custom-call(bf16[16,32,512]{2,1,0:T(8,128)(2,1)} %all-to-all-done.3.shares_ref, bf16[16,32,128]{2,1,0:T(8,128)(2,1)} %values.1.v_ref), custom_call_target="tpu_custom_call" | custom-call | tf_op jit(solution)/shard_map/share/pallas_call | solution.py:330
  128.3 6.5 %all-to-all-start.4 = ((bf16[16,32,640]{2,1,0:T(8,128)(2,1)}), bf16[16,32,640]{2,1,0:T(8,128)(2,1)}, u32[]{:S(2)}, u32[]{:S(2)}) async-start(bf16[16,32,640]{2,1,0:T(8,128)(2,1)} %share.1), calls=%async_computation.4 | async-start | bytes 1310720 | tf_op jit(solution)/shard_map/all_to_all | solution.py:389
  134.8 7.6 %input_grad.1 = bf16[128,8192]{1,0:T(8,128)(2,1)} custom-call(s32[5]{0:T(128)} %stack.23.place_ref, bf16[128,512]{1,0:T(8,128)(2,1)} %get-tuple-element.80.grad_ref, bf16[1024,256]{1,0:T(8,128)(2,1)} %copy-done.2, bf16[1024,256]{1,0:T(8,128)(2,1)} %collective-permute-done.3.refs_1_, bf16[1024,256]{1,0:T(8,128)(2,1)} %collective-permute-done.6.refs_2_, ...), custom_call_target="tpu_custom_call" | custom-call | tf_op jit(solution)/shard_map/input_grad/pallas_call | solution.py:307
  142.4 3.5 %all-to-all-done.4.v_ref.share_ref = bf16[16,32,640]{2,1,0:T(8,128)(2,1)} async-done(((bf16[16,32,640]{2,1,0:T(8,128)(2,1)}), bf16[16,32,640]{2,1,0:T(8,128)(2,1)}, u32[]{:S(2)}, u32[]{:S(2)}) %all-to-all-start.4) | async-done | bytes 655392 | tf_op jit(solution)/shard_map/all_to_all | solution.py:389
  145.9 5.2 %attend.1 = (bf16[128,4096]{1,0:T(8,128)(2,1)}, bf16[128,4096]{1,0:T(8,128)(2,1)}, bf16[128,512]{1,0:T(8,128)(2,1)}, f32[512,512]{1,0:T(8,128)}) custom-call(f32[128,4096]{1,0:T(8,128)} %get-tuple-element.49.probs_ref, bf16[128,4608]{1,0:T(8,128)(2,1)} %bitcast.9, bf16[128,4608]{1,0:T(8,128)(2,1)} %bitcast.10, ...), custom_call_target="tpu_custom_call" | custom-call | tf_op jit(solution)/shard_map/attend/pallas_call | solution.py:205
  (59 shorter events, 9.2 us)
Async XLA Ops:
  1.6 8.8 %collective-permute-start = (bf16[512,256]{1,0:T(8,128)(2,1)S(1)}, bf16[512,256]{1,0:T(8,128)(2,1)S(1)}, u32[]{:S(2)}, u32[]{:S(2)}) collective-permute-start(bf16[512,256]{1,0:T(8,128)(2,1)S(1)} %constant_dynamic-slice_fusion), channel_id=1, source_target_pairs={{0,1},{1,0},{2,3},{3,2},{4,5},{5,4},{6,7},{7,6},{8,9},{9,8},{10,11... | collective-permute-start | bytes 786440 | tf_op jit(solution)/shard_map/ppermute | solution.py:349
  5.4 44.4 %collective-permute-start.4 = (bf16[128,8192]{1,0:T(8,128)(2,1)}, bf16[128,8192]{1,0:T(8,128)(2,1)}, u32[]{:S(2)}, u32[]{:S(2)}) collective-permute-start(bf16[128,8192]{1,0:T(8,128)(2,1)} %x_ref.3), channel_id=1, source_target_pairs={{0,16},{16,0},{1,17},{17,1},{2,18},{18,2},{3,19},{19,3},{4,20},{20... | collective-permute-start | bytes 6291464 | tf_op jit(solution)/shard_map/ppermute | solution.py:350
  6.4 3.7 %collective-permute-start.1 = (s32[1,128]{1,0:T(1,128)}, s32[1,128]{1,0:T(1,128)S(1)}, u32[]{:S(2)}, u32[]{:S(2)}) collective-permute-start(s32[1,128]{1,0:T(1,128)} %order_ref.5), channel_id=1, source_target_pairs={{0,16},{16,0},{1,17},{17,1},{2,18},{18,2},{3,19},{19,3},{4,20},{20... | collective-permute-start | bytes 1544 | tf_op jit(solution)/shard_map/ppermute | solution.py:351
  10.1 19.3 %copy-start.14 = (s32[1,128]{1,0:T(1,128)}, s32[1,128]{1,0:T(1,128)S(1)}, u32[]{:S(2)}) copy-start(s32[1,128]{1,0:T(1,128)S(1)} %collective-permute-done.1.order_ref) | copy-start | bytes 1540
  10.4 25.6 %all-to-all-start = ((bf16[16,8,4608]{2,1,0:T(8,128)(2,1)}), bf16[16,8,4608]{2,1,0:T(8,128)(2,1)S(1)}, u32[]{:S(2)}, u32[]{:S(2)}) async-start(bf16[16,8,4608]{2,1,0:T(8,128)(2,1)} %bitcast.11), calls=%async_computation | async-start | bytes 2359296 | tf_op jit(solution)/shard_map/all_to_all | solution.py:355
  18.1 82.3 %copy-start.2 = (bf16[1024,256]{1,0:T(8,128)(2,1)}, bf16[1024,256]{1,0:T(8,128)(2,1)S(1)}, u32[]{:S(2)}) copy-start(bf16[1024,256]{1,0:T(8,128)(2,1)S(1)} %pad_maximum_fusion.refs_0_) | copy-start | bytes 1572868
  18.1 17.8 %collective-permute-start.2 = (bf16[1024,256]{1,0:T(8,128)(2,1)S(1)}, bf16[1024,256]{1,0:T(8,128)(2,1)S(1)}, u32[]{:S(2)}, u32[]{:S(2)}) collective-permute-start(bf16[1024,256]{1,0:T(8,128)(2,1)S(1)} %pad_maximum_fusion.refs_0_), channel_id=1, source_target_pairs={{0,2},{2,4},{4,6},{6,8},{8,10},{10,12},{12,14},{14,0},{1,3},{3,5},... | collective-permute-start | bytes 1572872 | tf_op jit(solution)/shard_map/ppermute | solution.py:360
  19.9 16.1 %collective-permute-start.3 = (bf16[1024,256]{1,0:T(8,128)(2,1)S(1)}, bf16[1024,256]{1,0:T(8,128)(2,1)}, u32[]{:S(2)}, u32[]{:S(2)}) collective-permute-start(bf16[1024,256]{1,0:T(8,128)(2,1)S(1)} %pad_maximum_fusion.refs_0_), channel_id=1, source_target_pairs={{0,14},{2,0},{4,2},{6,4},{8,6},{10,8},{12,10},{14,12},{1,15},{3,1}... | collective-permute-start | bytes 1572872 | tf_op jit(solution)/shard_map/ppermute | solution.py:361
  36.0 73.8 %copy-start.3 = (bf16[1024,256]{1,0:T(8,128)(2,1)}, bf16[1024,256]{1,0:T(8,128)(2,1)S(1)}, u32[]{:S(2)}) copy-start(bf16[1024,256]{1,0:T(8,128)(2,1)S(1)} %collective-permute-done.2.refs_7_) | copy-start | bytes 1572868
  36.0 9.2 %copy-start = (bf16[16,8,4608]{2,1,0:T(8,128)(2,1)}, bf16[16,8,4608]{2,1,0:T(8,128)(2,1)S(1)}, u32[]{:S(2)}) copy-start(bf16[16,8,4608]{2,1,0:T(8,128)(2,1)S(1)} %all-to-all-done) | copy-start | bytes 3538948
  36.0 21.4 %all-to-all-start.1 = ((bf16[8,128,512]{2,1,0:T(8,128)(2,1)}), bf16[8,128,512]{2,1,0:T(8,128)(2,1)}, u32[]{:S(2)}, u32[]{:S(2)}) async-start(bf16[8,128,512]{2,1,0:T(8,128)(2,1)} %sort_own.1), calls=%async_computation.1 | async-start | bytes 2097152 | tf_op jit(solution)/shard_map/all_to_all | solution.py:363
  40.9 15.7 %collective-permute-start.5 = (bf16[1024,256]{1,0:T(8,128)(2,1)S(1)}, bf16[1024,256]{1,0:T(8,128)(2,1)S(1)}, u32[]{:S(2)}, u32[]{:S(2)}) collective-permute-start(bf16[1024,256]{1,0:T(8,128)(2,1)S(1)} %collective-permute-done.2.refs_7_), channel_id=1, source_target_pairs={{0,2},{2,4},{4,6},{6,8},{8,10},{10,12},{12,14},{14,0},{1,3},{3,5},... | collective-permute-start | bytes 1572872 | tf_op jit(solution)/shard_map/ppermute | solution.py:364
  41.1 16.3 %collective-permute-start.6 = (bf16[1024,256]{1,0:T(8,128)(2,1)}, bf16[1024,256]{1,0:T(8,128)(2,1)}, u32[]{:S(2)}, u32[]{:S(2)}) collective-permute-start(bf16[1024,256]{1,0:T(8,128)(2,1)} %collective-permute-done.3.refs_1_), channel_id=1, source_target_pairs={{0,14},{2,0},{4,2},{6,4},{8,6},{10,8},{12,10},{14,12},{1,15},{3,1}... | collective-permute-start | bytes 1572872 | tf_op jit(solution)/shard_map/ppermute | solution.py:365
  57.4 33.7 %all-to-all-start.2 = ((bf16[8,256,512]{2,1,0:T(8,128)(2,1)}), bf16[8,256,512]{2,1,0:T(8,128)(2,1)S(1)}, u32[]{:S(2)}, u32[]{:S(2)}) async-start(bf16[8,256,512]{2,1,0:T(8,128)(2,1)} %sort_other.1), calls=%async_computation.2 | async-start | bytes 4194304 | tf_op jit(solution)/shard_map/all_to_all | solution.py:370
  62.0 12.8 %collective-permute-start.7 = (bf16[1024,256]{1,0:T(8,128)(2,1)}, bf16[1024,256]{1,0:T(8,128)(2,1)S(1)}, u32[]{:S(2)}, u32[]{:S(2)}) collective-permute-start(bf16[1024,256]{1,0:T(8,128)(2,1)} %copy-done.4), channel_id=1, source_target_pairs={{0,2},{2,4},{4,6},{6,8},{8,10},{10,12},{12,14},{14,0},{1,3},{3,5},... | collective-permute-start | bytes 1572872 | tf_op jit(solution)/shard_map/ppermute | solution.py:371
  62.0 12.8 %collective-permute-start.9 = (bf16[1024,256]{1,0:T(8,128)(2,1)}, bf16[1024,256]{1,0:T(8,128)(2,1)S(1)}, u32[]{:S(2)}, u32[]{:S(2)}) collective-permute-start(bf16[1024,256]{1,0:T(8,128)(2,1)} %collective-permute-done.6.refs_2_), channel_id=1, source_target_pairs={{0,14},{2,0},{4,2},{6,4},{8,6},{10,8},{12,10},{14,12},{1,15},{3,1}... | collective-permute-start | bytes 1572872 | tf_op jit(solution)/shard_map/ppermute | solution.py:372
  74.7 11.8 %collective-permute-start.8 = (bf16[1024,256]{1,0:T(8,128)(2,1)S(1)}, bf16[1024,256]{1,0:T(8,128)(2,1)}, u32[]{:S(2)}, u32[]{:S(2)}) collective-permute-start(bf16[1024,256]{1,0:T(8,128)(2,1)S(1)} %collective-permute-done.7.refs_5_), channel_id=1, source_target_pairs={{0,2},{2,4},{4,6},{6,8},{8,10},{10,12},{12,14},{14,0},{1,3},{3,5},... | collective-permute-start | bytes 1572872 | tf_op jit(solution)/shard_map/ppermute | solution.py:373
  91.1 4.8 %copy-start.1 = (bf16[8,256,512]{2,1,0:T(8,128)(2,1)}, bf16[8,256,512]{2,1,0:T(8,128)(2,1)S(1)}, u32[]{:S(2)}) copy-start(bf16[8,256,512]{2,1,0:T(8,128)(2,1)S(1)} %all-to-all-done.2.both_ref) | copy-start | bytes 6291460
  91.2 4.7 %collective-permute-start.10 = (bf16[8,128,512]{2,1,0:T(8,128)(2,1)S(1)}, bf16[8,128,512]{2,1,0:T(8,128)(2,1)}, u32[]{:S(2)}, u32[]{:S(2)}) collective-permute-start(bf16[8,128,512]{2,1,0:T(8,128)(2,1)S(1)} %slice.3), channel_id=1, source_target_pairs={{0,16},{16,0},{1,17},{17,1},{2,18},{18,2},{3,19},{19,3},{4,20},{20... | collective-permute-start | bytes 3145736 | tf_op jit(solution)/shard_map/ppermute | solution.py:375
  100.4 8.8 %collective-permute-start.11 = (bf16[1024,256]{1,0:T(8,128)(2,1)S(1)}, bf16[1024,256]{1,0:T(8,128)(2,1)S(1)}, u32[]{:S(2)}, u32[]{:S(2)}) collective-permute-start(bf16[1024,256]{1,0:T(8,128)(2,1)S(1)} %pad_maximum_fusion.refs_0_), channel_id=1, source_target_pairs={{0,16},{16,0},{1,17},{17,1},{2,18},{18,2},{3,19},{19,3},{4,20},{20... | collective-permute-start | bytes 1572872 | tf_op jit(solution)/shard_map/ppermute | solution.py:381
  100.7 8.9 %collective-permute-start.12 = (bf16[1024,256]{1,0:T(8,128)(2,1)}, bf16[1024,256]{1,0:T(8,128)(2,1)S(1)}, u32[]{:S(2)}, u32[]{:S(2)}) collective-permute-start(bf16[1024,256]{1,0:T(8,128)(2,1)} %collective-permute-done.3.refs_1_), channel_id=1, source_target_pairs={{0,16},{16,0},{1,17},{17,1},{2,18},{18,2},{3,19},{19,3},{4,20},{20... | collective-permute-start | bytes 1572872 | tf_op jit(solution)/shard_map/ppermute | solution.py:381
  100.9 8.9 %collective-permute-start.13 = (bf16[1024,256]{1,0:T(8,128)(2,1)}, bf16[1024,256]{1,0:T(8,128)(2,1)S(1)}, u32[]{:S(2)}, u32[]{:S(2)}) collective-permute-start(bf16[1024,256]{1,0:T(8,128)(2,1)} %collective-permute-done.6.refs_2_), channel_id=1, source_target_pairs={{0,16},{16,0},{1,17},{17,1},{2,18},{18,2},{3,19},{19,3},{4,20},{20... | collective-permute-start | bytes 1572872 | tf_op jit(solution)/shard_map/ppermute | solution.py:381
  101.3 25.1 %all-to-all-start.3 = ((bf16[16,32,512]{2,1,0:T(8,128)(2,1)}), bf16[16,32,512]{2,1,0:T(8,128)(2,1)}, u32[]{:S(2)}, u32[]{:S(2)}) async-start(bf16[16,32,512]{2,1,0:T(8,128)(2,1)} %weight_part.1), calls=%async_computation.3 | async-start | bytes 1048576 | tf_op jit(solution)/shard_map/all_to_all | solution.py:378
  108.6 2.3 %collective-permute-start.14 = (bf16[1024,256]{1,0:T(8,128)(2,1)}, bf16[1024,256]{1,0:T(8,128)(2,1)S(1)}, u32[]{:S(2)}, u32[]{:S(2)}) collective-permute-start(bf16[1024,256]{1,0:T(8,128)(2,1)} %copy-done.6), channel_id=1, source_target_pairs={{0,16},{16,0},{1,17},{17,1},{2,18},{18,2},{3,19},{19,3},{4,20},{20... | collective-permute-start | bytes 1572872 | tf_op jit(solution)/shard_map/ppermute | solution.py:381
  109.1 2.5 %collective-permute-start.15 = (bf16[1024,256]{1,0:T(8,128)(2,1)}, bf16[1024,256]{1,0:T(8,128)(2,1)S(1)}, u32[]{:S(2)}, u32[]{:S(2)}) collective-permute-start(bf16[1024,256]{1,0:T(8,128)(2,1)} %collective-permute-done.8.refs_4_), channel_id=1, source_target_pairs={{0,16},{16,0},{1,17},{17,1},{2,18},{18,2},{3,19},{19,3},{4,20},{20... | collective-permute-start | bytes 1572872 | tf_op jit(solution)/shard_map/ppermute | solution.py:381
  109.2 3.9 %collective-permute-start.16 = (bf16[1024,256]{1,0:T(8,128)(2,1)}, bf16[1024,256]{1,0:T(8,128)(2,1)S(1)}, u32[]{:S(2)}, u32[]{:S(2)}) collective-permute-start(bf16[1024,256]{1,0:T(8,128)(2,1)} %copy-done.5), channel_id=1, source_target_pairs={{0,16},{16,0},{1,17},{17,1},{2,18},{18,2},{3,19},{19,3},{4,20},{20... | collective-permute-start | bytes 1572872 | tf_op jit(solution)/shard_map/ppermute | solution.py:381
  109.6 4.2 %collective-permute-start.17 = (bf16[1024,256]{1,0:T(8,128)(2,1)}, bf16[1024,256]{1,0:T(8,128)(2,1)S(1)}, u32[]{:S(2)}, u32[]{:S(2)}) collective-permute-start(bf16[1024,256]{1,0:T(8,128)(2,1)} %copy-done.4), channel_id=1, source_target_pairs={{0,16},{16,0},{1,17},{17,1},{2,18},{18,2},{3,19},{19,3},{4,20},{20... | collective-permute-start | bytes 1572872 | tf_op jit(solution)/shard_map/ppermute | solution.py:381
  109.7 1.9 %copy-start.9 = (bf16[1024,256]{1,0:T(8,128)(2,1)}, bf16[1024,256]{1,0:T(8,128)(2,1)S(1)}, u32[]{:S(2)}) copy-start(bf16[1024,256]{1,0:T(8,128)(2,1)S(1)} %collective-permute-done.13.refs_10_) | copy-start | bytes 1572868
  109.7 5.0 %collective-permute-start.18 = (bf16[1024,256]{1,0:T(8,128)(2,1)S(1)}, bf16[1024,256]{1,0:T(8,128)(2,1)}, u32[]{:S(2)}, u32[]{:S(2)}) collective-permute-start(bf16[1024,256]{1,0:T(8,128)(2,1)S(1)} %collective-permute-done.2.refs_7_), channel_id=1, source_target_pairs={{0,16},{16,0},{1,17},{17,1},{2,18},{18,2},{3,19},{19,3},{4,20},{20... | collective-permute-start | bytes 1572872 | tf_op jit(solution)/shard_map/ppermute | solution.py:381
  110.9 2.2 %copy-start.10 = (bf16[1024,256]{1,0:T(8,128)(2,1)}, bf16[1024,256]{1,0:T(8,128)(2,1)S(1)}, u32[]{:S(2)}) copy-start(bf16[1024,256]{1,0:T(8,128)(2,1)S(1)} %collective-permute-done.14.refs_11_) | copy-start | bytes 1572868
  111.6 2.2 %copy-start.11 = (bf16[1024,256]{1,0:T(8,128)(2,1)}, bf16[1024,256]{1,0:T(8,128)(2,1)S(1)}, u32[]{:S(2)}) copy-start(bf16[1024,256]{1,0:T(8,128)(2,1)S(1)} %collective-permute-done.15.refs_12_) | copy-start | bytes 1572868
  128.3 17.5 %all-to-all-start.4 = ((bf16[16,32,640]{2,1,0:T(8,128)(2,1)}), bf16[16,32,640]{2,1,0:T(8,128)(2,1)}, u32[]{:S(2)}, u32[]{:S(2)}) async-start(bf16[16,32,640]{2,1,0:T(8,128)(2,1)} %share.1), calls=%async_computation.4 | async-start | bytes 1310720 | tf_op jit(solution)/shard_map/all_to_all | solution.py:389
  (7 other events, 6.3 us)
